TPU v7x, 256 devices: a whole 4x4x8 slice. The times are simulated.
256 devices in a mesh: gx: 16 (over y, x), gy: 16 (over z, core).
Axes of the slice: x: 4, y: 4, z: 8, core: 2. Of those that a mesh axis runs over, the one named last changes fastest.
Arguments:
- right_side: float32 [128, 256, 192], P('gx', 'gy'), may hold values from -13 to 13
- phase: int32 [128, 256, 192], P('gx', 'gy'), may hold values 0 or 1
Outputs:
- pressure: float32 [128, 256, 192], P('gx', 'gy')
- residual: float32 [128, 256, 192], P('gx', 'gy')
All inputs are finite; a program needn't handle non-finite values. No bound on the sum of `phase` on one device may be relied on, other than what follows from the above.
Results may differ from a plain program's by a relative error of at most 0.0003.
Values sent between devices are 32-bit elements; how exact they have to be, the bound alone decides.
A program may use at most 128 MiB of HBM per device.

v0:
```python
import jax
import jax.numpy as jnp
from jax import lax
from jax.sharding import PartitionSpec as P

PRE = 2
BOTTOM = 8


def extended(cells, sides, width):
    for axis, dim in sides:
        count = lax.axis_size(axis)
        ends = count - 1
        head = lax.slice_in_dim(cells, 0, width, axis=dim)
        tail = lax.slice_in_dim(cells, cells.shape[dim] - width, cells.shape[dim], axis=dim)
        cells = jnp.concatenate(
            [
                lax.ppermute(tail, axis, [(i, (i + 1) % count) for i in range(ends)]),
                cells,
                lax.ppermute(head, axis, [((i + 1) % count, i) for i in range(ends)]),
            ],
            axis=dim,
        )
    return cells


def parity(shape):
    total = lax.broadcasted_iota(jnp.int32, shape, 0) + lax.broadcasted_iota(jnp.int32, shape, 1)
    return (total + lax.broadcasted_iota(jnp.int32, shape, 2)) % 2


def harmonic(first, second):
    return 2.0 * first * second / (first + second)


def weights_of(beta_grown):
    center = beta_grown[1:-1, 1:-1, 1:-1]
    return jnp.stack(
        [
            harmonic(center, beta_grown[:-2, 1:-1, 1:-1]),
            harmonic(center, beta_grown[2:, 1:-1, 1:-1]),
            harmonic(center, beta_grown[1:-1, :-2, 1:-1]),
            harmonic(center, beta_grown[1:-1, 2:, 1:-1]),
            harmonic(center, beta_grown[1:-1, 1:-1, :-2]),
            harmonic(center, beta_grown[1:-1, 1:-1, 2:]),
        ],
        0,
    )


def diagonal_of(weights):
    return weights[0] + weights[1] + weights[2] + weights[3] + weights[4] + weights[5]


def neighbor_sum(full, weights):
    total = weights[0] * full[:-2, 1:-1, 1:-1]
    total = total + weights[1] * full[2:, 1:-1, 1:-1]
    total = total + weights[2] * full[1:-1, :-2, 1:-1]
    total = total + weights[3] * full[1:-1, 2:, 1:-1]
    total = total + weights[4] * full[1:-1, 1:-1, :-2]
    return total + weights[5] * full[1:-1, 1:-1, 2:]


def blocks_of(field):
    sx, sy, sz = field.shape
    return field.reshape(sx // 2, 2, sy // 2, 2, sz // 2, 2)


def face_average(block, axis, side):
    parts = []
    for first in (0, 1):
        for second in (0, 1):
            for third in (0, 1):
                pick = (first, second, third)
                if pick[axis] == side:
                    parts.append(block[:, first, :, second, :, third])
    return (parts[0] + parts[1] + (parts[2] + parts[3])) * 0.25


def coarsen(weights):
    return jnp.stack([face_average(blocks_of(weights[c]), c // 2, c % 2) for c in range(6)], 0)


def restrict(field):
    block = blocks_of(field)
    parts = [block[:, a, :, b, :, c] for a in (0, 1) for b in (0, 1) for c in (0, 1)]
    return (
        parts[0] + parts[1] + (parts[2] + parts[3]) + (parts[4] + parts[5] + (parts[6] + parts[7]))
    ) * 0.125


def prolong(field):
    return jnp.repeat(jnp.repeat(jnp.repeat(field, 2, 0), 2, 1), 2, 2)


def update(grown, source, weights, diagonal, scale, color):
    full = jnp.pad(grown, ((0, 0), (0, 0), (1, 1)))
    center = full[1:-1, 1:-1, 1:-1]
    fresh = (scale * source + neighbor_sum(full, weights)) / diagonal
    return jnp.where(parity(center.shape) == color, fresh, center)


def grow(field):
    return extended(field, (("gx", 0), ("gy", 1)), 1)


def relax_plain(field, source, weights, diagonal, scale, count):
    for sweep in range(count):
        for color in (0, 1):
            field = update(grow(field), source, weights, diagonal, scale, color)
    return field


def smooth(field, source, weights, diagonal, scale, count):
    return relax_plain(field, source, weights, diagonal, scale, count)


def residual_of(field, source, weights, diagonal, inverse):
    full = jnp.pad(grow(field), ((0, 0), (0, 0), (1, 1)))
    center = full[1:-1, 1:-1, 1:-1]
    return source - (diagonal * center - neighbor_sum(full, weights)) * inverse


def coarse_solve(source, weights, diagonal):
    return smooth(jnp.zeros_like(source), source, weights, diagonal, 16.0, BOTTOM)


def local(right_side, phase):
    grown_phase = extended(phase, (("gx", 0), ("gy", 1)), 1)
    padded_phase = jnp.pad(grown_phase, ((0, 0), (0, 0), (1, 1)))
    beta = jnp.where(padded_phase == 1, 0.1, 1.0).astype(jnp.float32)
    fine_w = weights_of(beta)
    mid_w = coarsen(fine_w)
    low_w = coarsen(mid_w)
    fine_d, mid_d, low_d = (diagonal_of(fine_w), diagonal_of(mid_w), diagonal_of(low_w))
    fine_p = smooth(jnp.zeros_like(right_side), right_side, fine_w, fine_d, 1.0, PRE)
    mid_b = restrict(residual_of(fine_p, right_side, fine_w, fine_d, 1.0))
    mid_p = smooth(jnp.zeros_like(mid_b), mid_b, mid_w, mid_d, 4.0, PRE)
    low_b = restrict(residual_of(mid_p, mid_b, mid_w, mid_d, 0.25))
    low_p = coarse_solve(low_b, low_w, low_d)
    mid_p = smooth(mid_p + prolong(low_p), mid_b, mid_w, mid_d, 4.0, PRE)
    pressure = smooth(fine_p + prolong(mid_p), right_side, fine_w, fine_d, 1.0, PRE)
    residual = residual_of(pressure, right_side, fine_w, fine_d, 1.0)
    return (pressure, residual)


def solution(mesh):
    in_specs = (P("gx", "gy", None), P("gx", "gy", None))
    out_specs = (P("gx", "gy", None), P("gx", "gy", None))
    return jax.shard_map(local, mesh=mesh, in_specs=in_specs, out_specs=out_specs, check_vma=False)
```

profile of v0, /device:TPU:103, one launch (start us, length us, event | category | flops | bytes accessed | tf_op | source)
XLA Modules:
  0.0 783.0 jit_solution(5961765220588175173)
XLA Ops:
  6.1 5.2 collective-permute-start.44
  13.3 5.5 collective-permute-start.24
  21.4 5.5 collective-permute-start
  34.6 9.0 %collective-permute-start.46 = (f32[4,1,48]{2,1,0:T(1,128)S(1)}, f32[4,1,48]{2,1,0:T(1,128)S(1)}, u32[]{:S(2)}, u32[]{:S(2)}) collective-permute-start(f32[4,1,48]{2,1,0:T(1,128)S(1)} %get-tuple-element.185), channel_id=1, source_target_pairs={{0,1},{1,2},{2,3},{3,4},{4,5},{5,6},{6,7},{7,8},{8,9},{9,10},{10,1... | collective-permute-start | bytes 2312 | tf_op jit(solution)/shard_map/ppermute | solution.py:18
  48.1 4.4 collective-permute-start.6
  69.9 4.9 collective-permute-start.10
  76.8 8.1 %reshape_squeeze_stack.24 = f32[4,2,8,2,96,2]{5,4,3,2,1,0:T(8,128)} reshape(f32[8,16,192]{2,1,0:T(8,128)S(1)} %get-tuple-element.26) | data formatting | bytes 196608 | tf_op jit(solution)/shard_map/reshape;squeeze;stack | solution.py:66
  85.2 5.8 collective-permute-start.12
  92.9 6.0 fusion.443
  98.9 8.0 %reshape_squeeze_stack.25 = f32[4,2,8,2,96,2]{5,4,3,2,1,0:T(8,128)} reshape(f32[8,16,192]{2,1,0:T(8,128)S(1)} %get-tuple-element.25) | data formatting | bytes 196608 | tf_op jit(solution)/shard_map/reshape;squeeze;stack | solution.py:66
  106.9 5.1 collective-permute-start.14
  114.0 6.5 fusion.442
  120.5 8.0 %reshape_squeeze_stack.26 = f32[4,2,8,2,96,2]{5,4,3,2,1,0:T(8,128)} reshape(f32[8,16,192]{2,1,0:T(8,128)S(1)} %get-tuple-element.27) | data formatting | bytes 196608 | tf_op jit(solution)/shard_map/reshape;squeeze;stack | solution.py:66
  128.9 5.8 collective-permute-start.16
  136.7 6.5 fusion.441
  143.3 8.0 %reshape_squeeze_stack.27 = f32[4,2,8,2,96,2]{5,4,3,2,1,0:T(8,128)} reshape(f32[8,16,192]{2,1,0:T(8,128)S(1)} %get-tuple-element.28) | data formatting | bytes 196608 | tf_op jit(solution)/shard_map/reshape;squeeze;stack | solution.py:66
  151.3 5.1 collective-permute-start.18
  158.4 6.5 fusion.440
  164.8 8.0 %reshape_squeeze_stack.28 = f32[4,2,8,2,96,2]{5,4,3,2,1,0:T(8,128)} reshape(f32[8,16,192]{2,1,0:T(8,128)S(1)} %get-tuple-element.29) | data formatting | bytes 196608 | tf_op jit(solution)/shard_map/reshape;squeeze;stack | solution.py:66
  173.3 5.8 collective-permute-start.20
  181.0 5.6 fusion.439
  186.5 8.0 %reshape_squeeze_stack.29 = f32[4,2,8,2,96,2]{5,4,3,2,1,0:T(8,128)} reshape(f32[8,16,192]{2,1,0:T(8,128)S(1)} %get-tuple-element.30) | data formatting | bytes 196608 | tf_op jit(solution)/shard_map/reshape;squeeze;stack | solution.py:66
  194.6 5.1 collective-permute-start.22
  201.9 7.1 fusion.438
  247.3 8.5 %reshape.162 = f32[4,2,8,2,96,2]{5,4,3,2,1,0:T(8,128)} reshape(f32[8,16,192]{2,1,0:T(8,128)S(1)} %fusion.81) | data formatting | bytes 196608 | tf_op jit(solution)/shard_map/reshape | solution.py:66
  255.7 8.0 %multiply_reduce_fusion = (f32[4,8,96]{2,1,0:T(8,128)S(1)}, f32[4,8,96]{2,1,0:T(8,128)S(1)}) fusion(f32[4,2,8,2,96,2]{5,4,3,2,1,0:T(8,128)} %reshape.162), kind=kLoop, calls=%fused_computation.7 | loop fusion | flops 27648 | bytes 122880 | tf_op jit(solution)/shard_map/mul | solution.py:87
  263.9 5.8 collective-permute-start.28
  276.1 6.3 collective-permute-start.30
  357.8 6.0 collective-permute-start.50
  704.6 4.3 collective-permute-done.127
  741.1 4.3 collective-permute-done.135
  759.3 4.3 collective-permute-done.139
  (527 shorter events, 579.0 us)
Async XLA Ops:
  0.6 43.0 %collective-permute-start.4 = (f32[1,16,192]{2,1,0:T(8,128)S(1)}, f32[1,16,192]{2,1,0:T(8,128)S(1)}, u32[]{:S(2)}, u32[]{:S(2)}) collective-permute-start(f32[1,16,192]{2,1,0:T(8,128)S(1)} %broadcast.196), channel_id=1, source_target_pairs={{0,16},{16,32},{32,48},{48,64},{64,80},{80,96},{96,112},{112,128},... | collective-permute-start | bytes 36872 | tf_op jit(solution)/shard_map/ppermute | solution.py:18
  3.9 41.7 %collective-permute-start.5 = (f32[1,16,192]{2,1,0:T(8,128)S(1)}, f32[1,16,192]{2,1,0:T(8,128)S(1)}, u32[]{:S(2)}, u32[]{:S(2)}) collective-permute-start(f32[1,16,192]{2,1,0:T(8,128)S(1)} %broadcast.196), channel_id=1, source_target_pairs={{16,0},{32,16},{48,32},{64,48},{80,64},{96,80},{112,96},{128,112},... | collective-permute-start | bytes 36872 | tf_op jit(solution)/shard_map/ppermute | solution.py:20
  6.1 13.4 %collective-permute-start.44 = (f32[1,4,48]{2,1,0:T(4,128)S(1)}, f32[1,4,48]{2,1,0:T(4,128)S(1)}, u32[]{:S(2)}, u32[]{:S(2)}) collective-permute-start(f32[1,4,48]{2,1,0:T(4,128)S(1)} %broadcast.203), channel_id=1, source_target_pairs={{0,16},{16,32},{32,48},{48,64},{64,80},{80,96},{96,112},{112,128},... | collective-permute-start | bytes 2312 | tf_op jit(solution)/shard_map/ppermute | solution.py:18
  11.3 10.1 %collective-permute-start.45 = (f32[1,4,48]{2,1,0:T(4,128)S(1)}, f32[1,4,48]{2,1,0:T(4,128)S(1)}, u32[]{:S(2)}, u32[]{:S(2)}) collective-permute-start(f32[1,4,48]{2,1,0:T(4,128)S(1)} %broadcast.203), channel_id=1, source_target_pairs={{16,0},{32,16},{48,32},{64,48},{80,64},{96,80},{112,96},{128,112},... | collective-permute-start | bytes 2312 | tf_op jit(solution)/shard_map/ppermute | solution.py:20
  13.3 49.6 %collective-permute-start.24 = (f32[1,8,96]{2,1,0:T(8,128)S(1)}, f32[1,8,96]{2,1,0:T(8,128)S(1)}, u32[]{:S(2)}, u32[]{:S(2)}) collective-permute-start(f32[1,8,96]{2,1,0:T(8,128)S(1)} %broadcast.199), channel_id=1, source_target_pairs={{0,16},{16,32},{32,48},{48,64},{64,80},{80,96},{96,112},{112,128},... | collective-permute-start | bytes 9224 | tf_op jit(solution)/shard_map/ppermute | solution.py:18
  19.5 45.3 %collective-permute-start.25 = (f32[1,8,96]{2,1,0:T(8,128)S(1)}, f32[1,8,96]{2,1,0:T(8,128)S(1)}, u32[]{:S(2)}, u32[]{:S(2)}) collective-permute-start(f32[1,8,96]{2,1,0:T(8,128)S(1)} %broadcast.199), channel_id=1, source_target_pairs={{16,0},{32,16},{48,32},{64,48},{80,64},{96,80},{112,96},{128,112},... | collective-permute-start | bytes 9224 | tf_op jit(solution)/shard_map/ppermute | solution.py:20
  34.6 237.0 %collective-permute-start.46 = (f32[4,1,48]{2,1,0:T(1,128)S(1)}, f32[4,1,48]{2,1,0:T(1,128)S(1)}, u32[]{:S(2)}, u32[]{:S(2)}) collective-permute-start(f32[4,1,48]{2,1,0:T(1,128)S(1)} %get-tuple-element.185), channel_id=1, source_target_pairs={{0,1},{1,2},{2,3},{3,4},{4,5},{5,6},{6,7},{7,8},{8,9},{9,10},{10,1... | collective-permute-start | bytes 2312 | tf_op jit(solution)/shard_map/ppermute | solution.py:18
  45.6 6.8 collective-permute-start.3
  54.6 217.0 %collective-permute-start.47 = (f32[4,1,48]{2,1,0:T(1,128)S(1)}, f32[4,1,48]{2,1,0:T(1,128)S(1)}, u32[]{:S(2)}, u32[]{:S(2)}) collective-permute-start(f32[4,1,48]{2,1,0:T(1,128)S(1)} %get-tuple-element.186), channel_id=1, source_target_pairs={{1,0},{2,1},{3,2},{4,3},{5,4},{6,5},{7,6},{8,7},{9,8},{10,9},{11,1... | collective-permute-start | bytes 2312 | tf_op jit(solution)/shard_map/ppermute | solution.py:20
  59.2 8.6 %collective-permute-start.8 = (f32[1,16,192]{2,1,0:T(8,128)S(1)}, f32[1,16,192]{2,1,0:T(8,128)S(1)}, u32[]{:S(2)}, u32[]{:S(2)}) collective-permute-start(f32[1,16,192]{2,1,0:T(8,128)S(1)} %get-tuple-element.117), channel_id=1, source_target_pairs={{0,16},{16,32},{32,48},{48,64},{64,80},{80,96},{96,112},{112,128},... | collective-permute-start | bytes 36872 | tf_op jit(solution)/shard_map/ppermute | solution.py:18
  62.9 6.9 collective-permute-start.9
  64.9 9.8 %collective-permute-start.26 = (f32[6,1,96]{2,1,0:T(1,128)S(1)}, f32[6,1,96]{2,1,0:T(1,128)S(1)}, u32[]{:S(2)}, u32[]{:S(2)}) collective-permute-start(f32[6,1,96]{2,1,0:T(1,128)S(1)} %get-tuple-element.137), channel_id=1, source_target_pairs={{0,1},{1,2},{2,3},{3,4},{4,5},{5,6},{6,7},{7,8},{8,9},{9,10},{10,1... | collective-permute-start | bytes 6920 | tf_op jit(solution)/shard_map/ppermute | solution.py:18
  67.9 8.8 %collective-permute-start.27 = (f32[6,1,96]{2,1,0:T(1,128)S(1)}, f32[6,1,96]{2,1,0:T(1,128)S(1)}, u32[]{:S(2)}, u32[]{:S(2)}) collective-permute-start(f32[6,1,96]{2,1,0:T(1,128)S(1)} %get-tuple-element.138), channel_id=1, source_target_pairs={{1,0},{2,1},{3,2},{4,3},{5,4},{6,5},{7,6},{8,7},{9,8},{10,9},{11,1... | collective-permute-start | bytes 6920 | tf_op jit(solution)/shard_map/ppermute | solution.py:20
  69.9 15.0 %collective-permute-start.10 = (f32[10,1,192]{2,1,0:T(1,128)S(1)}, f32[10,1,192]{2,1,0:T(1,128)S(1)}, u32[]{:S(2)}, u32[]{:S(2)}) collective-permute-start(f32[10,1,192]{2,1,0:T(1,128)S(1)} %get-tuple-element.95), channel_id=1, source_target_pairs={{0,1},{1,2},{2,3},{3,4},{4,5},{5,6},{6,7},{7,8},{8,9},{9,10},{10,1... | collective-permute-start | bytes 23048 | tf_op jit(solution)/shard_map/ppermute | solution.py:18
  74.7 10.1 %collective-permute-start.11 = (f32[10,1,192]{2,1,0:T(1,128)S(1)}, f32[10,1,192]{2,1,0:T(1,128)S(1)}, u32[]{:S(2)}, u32[]{:S(2)}) collective-permute-start(f32[10,1,192]{2,1,0:T(1,128)S(1)} %get-tuple-element.96), channel_id=1, source_target_pairs={{1,0},{2,1},{3,2},{4,3},{5,4},{6,5},{7,6},{8,7},{9,8},{10,9},{11,1... | collective-permute-start | bytes 23048 | tf_op jit(solution)/shard_map/ppermute | solution.py:20
  85.2 21.7 %collective-permute-start.12 = (f32[1,16,192]{2,1,0:T(8,128)S(1)}, f32[1,16,192]{2,1,0:T(8,128)S(1)}, u32[]{:S(2)}, u32[]{:S(2)}) collective-permute-start(f32[1,16,192]{2,1,0:T(8,128)S(1)} %get-tuple-element.115), channel_id=1, source_target_pairs={{0,16},{16,32},{32,48},{48,64},{64,80},{80,96},{96,112},{112,128},... | collective-permute-start | bytes 36872 | tf_op jit(solution)/shard_map/ppermute | solution.py:18
  91.0 15.9 %collective-permute-start.13 = (f32[1,16,192]{2,1,0:T(8,128)S(1)}, f32[1,16,192]{2,1,0:T(8,128)S(1)}, u32[]{:S(2)}, u32[]{:S(2)}) collective-permute-start(f32[1,16,192]{2,1,0:T(8,128)S(1)} %get-tuple-element.116), channel_id=1, source_target_pairs={{16,0},{32,16},{48,32},{64,48},{80,64},{96,80},{112,96},{128,112},... | collective-permute-start | bytes 36872 | tf_op jit(solution)/shard_map/ppermute | solution.py:20
  106.9 21.6 %collective-permute-start.14 = (f32[10,1,192]{2,1,0:T(1,128)S(1)}, f32[10,1,192]{2,1,0:T(1,128)S(1)}, u32[]{:S(2)}, u32[]{:S(2)}) collective-permute-start(f32[10,1,192]{2,1,0:T(1,128)S(1)} %get-tuple-element.93), channel_id=1, source_target_pairs={{0,1},{1,2},{2,3},{3,4},{4,5},{5,6},{6,7},{7,8},{8,9},{9,10},{10,1... | collective-permute-start | bytes 23048 | tf_op jit(solution)/shard_map/ppermute | solution.py:18
  112.1 16.4 %collective-permute-start.15 = (f32[10,1,192]{2,1,0:T(1,128)S(1)}, f32[10,1,192]{2,1,0:T(1,128)S(1)}, u32[]{:S(2)}, u32[]{:S(2)}) collective-permute-start(f32[10,1,192]{2,1,0:T(1,128)S(1)} %get-tuple-element.94), channel_id=1, source_target_pairs={{1,0},{2,1},{3,2},{4,3},{5,4},{6,5},{7,6},{8,7},{9,8},{10,9},{11,1... | collective-permute-start | bytes 23048 | tf_op jit(solution)/shard_map/ppermute | solution.py:20
  128.9 22.4 %collective-permute-start.16 = (f32[1,16,192]{2,1,0:T(8,128)S(1)}, f32[1,16,192]{2,1,0:T(8,128)S(1)}, u32[]{:S(2)}, u32[]{:S(2)}) collective-permute-start(f32[1,16,192]{2,1,0:T(8,128)S(1)} %get-tuple-element.113), channel_id=1, source_target_pairs={{0,16},{16,32},{32,48},{48,64},{64,80},{80,96},{96,112},{112,128},... | collective-permute-start | bytes 36872 | tf_op jit(solution)/shard_map/ppermute | solution.py:18
  134.6 16.6 %collective-permute-start.17 = (f32[1,16,192]{2,1,0:T(8,128)S(1)}, f32[1,16,192]{2,1,0:T(8,128)S(1)}, u32[]{:S(2)}, u32[]{:S(2)}) collective-permute-start(f32[1,16,192]{2,1,0:T(8,128)S(1)} %get-tuple-element.114), channel_id=1, source_target_pairs={{16,0},{32,16},{48,32},{64,48},{80,64},{96,80},{112,96},{128,112},... | collective-permute-start | bytes 36872 | tf_op jit(solution)/shard_map/ppermute | solution.py:20
  151.3 21.6 %collective-permute-start.18 = (f32[10,1,192]{2,1,0:T(1,128)S(1)}, f32[10,1,192]{2,1,0:T(1,128)S(1)}, u32[]{:S(2)}, u32[]{:S(2)}) collective-permute-start(f32[10,1,192]{2,1,0:T(1,128)S(1)} %get-tuple-element.91), channel_id=1, source_target_pairs={{0,1},{1,2},{2,3},{3,4},{4,5},{5,6},{6,7},{7,8},{8,9},{9,10},{10,1... | collective-permute-start | bytes 23048 | tf_op jit(solution)/shard_map/ppermute | solution.py:18
  156.5 16.4 %collective-permute-start.19 = (f32[10,1,192]{2,1,0:T(1,128)S(1)}, f32[10,1,192]{2,1,0:T(1,128)S(1)}, u32[]{:S(2)}, u32[]{:S(2)}) collective-permute-start(f32[10,1,192]{2,1,0:T(1,128)S(1)} %get-tuple-element.92), channel_id=1, source_target_pairs={{1,0},{2,1},{3,2},{4,3},{5,4},{6,5},{7,6},{8,7},{9,8},{10,9},{11,1... | collective-permute-start | bytes 23048 | tf_op jit(solution)/shard_map/ppermute | solution.py:20
  173.3 21.3 %collective-permute-start.20 = (f32[1,16,192]{2,1,0:T(8,128)S(1)}, f32[1,16,192]{2,1,0:T(8,128)S(1)}, u32[]{:S(2)}, u32[]{:S(2)}) collective-permute-start(f32[1,16,192]{2,1,0:T(8,128)S(1)} %get-tuple-element.111), channel_id=1, source_target_pairs={{0,16},{16,32},{32,48},{48,64},{64,80},{80,96},{96,112},{112,128},... | collective-permute-start | bytes 36872 | tf_op jit(solution)/shard_map/ppermute | solution.py:18
  179.0 15.5 %collective-permute-start.21 = (f32[1,16,192]{2,1,0:T(8,128)S(1)}, f32[1,16,192]{2,1,0:T(8,128)S(1)}, u32[]{:S(2)}, u32[]{:S(2)}) collective-permute-start(f32[1,16,192]{2,1,0:T(8,128)S(1)} %get-tuple-element.112), channel_id=1, source_target_pairs={{16,0},{32,16},{48,32},{64,48},{80,64},{96,80},{112,96},{128,112},... | collective-permute-start | bytes 36872 | tf_op jit(solution)/shard_map/ppermute | solution.py:20
  194.6 52.3 %collective-permute-start.22 = (f32[10,1,192]{2,1,0:T(1,128)S(1)}, f32[10,1,192]{2,1,0:T(1,128)S(1)}, u32[]{:S(2)}, u32[]{:S(2)}) collective-permute-start(f32[10,1,192]{2,1,0:T(1,128)S(1)} %get-tuple-element.89), channel_id=1, source_target_pairs={{0,1},{1,2},{2,3},{3,4},{4,5},{5,6},{6,7},{7,8},{8,9},{9,10},{10,1... | collective-permute-start | bytes 23048 | tf_op jit(solution)/shard_map/ppermute | solution.py:18
  199.7 47.2 %collective-permute-start.23 = (f32[10,1,192]{2,1,0:T(1,128)S(1)}, f32[10,1,192]{2,1,0:T(1,128)S(1)}, u32[]{:S(2)}, u32[]{:S(2)}) collective-permute-start(f32[10,1,192]{2,1,0:T(1,128)S(1)} %get-tuple-element.90), channel_id=1, source_target_pairs={{1,0},{2,1},{3,2},{4,3},{5,4},{6,5},{7,6},{8,7},{9,8},{10,9},{11,1... | collective-permute-start | bytes 23048 | tf_op jit(solution)/shard_map/ppermute | solution.py:20
  263.9 8.2 %collective-permute-start.28 = (f32[1,8,96]{2,1,0:T(8,128)S(1)}, f32[1,8,96]{2,1,0:T(8,128)S(1)}, u32[]{:S(2)}, u32[]{:S(2)}) collective-permute-start(f32[1,8,96]{2,1,0:T(8,128)S(1)} %get-tuple-element.153), channel_id=1, source_target_pairs={{0,16},{16,32},{32,48},{48,64},{64,80},{80,96},{96,112},{112,128},... | collective-permute-start | bytes 9224 | tf_op jit(solution)/shard_map/ppermute | solution.py:18
  276.1 8.8 %collective-permute-start.30 = (f32[6,1,96]{2,1,0:T(1,128)S(1)}, f32[6,1,96]{2,1,0:T(1,128)S(1)}, u32[]{:S(2)}, u32[]{:S(2)}) collective-permute-start(f32[6,1,96]{2,1,0:T(1,128)S(1)} %get-tuple-element.135), channel_id=1, source_target_pairs={{0,1},{1,2},{2,3},{3,4},{4,5},{5,6},{6,7},{7,8},{8,9},{9,10},{10,1... | collective-permute-start | bytes 6920 | tf_op jit(solution)/shard_map/ppermute | solution.py:18
  332.8 15.5 %collective-permute-start.42 = (f32[6,1,96]{2,1,0:T(1,128)S(1)}, f32[6,1,96]{2,1,0:T(1,128)S(1)}, u32[]{:S(2)}, u32[]{:S(2)}) collective-permute-start(f32[6,1,96]{2,1,0:T(1,128)S(1)} %get-tuple-element.129), channel_id=1, source_target_pairs={{0,1},{1,2},{2,3},{3,4},{4,5},{5,6},{6,7},{7,8},{8,9},{9,10},{10,1... | collective-permute-start | bytes 6920 | tf_op jit(solution)/shard_map/ppermute | solution.py:18
  336.0 12.4 %collective-permute-start.43 = (f32[6,1,96]{2,1,0:T(1,128)S(1)}, f32[6,1,96]{2,1,0:T(1,128)S(1)}, u32[]{:S(2)}, u32[]{:S(2)}) collective-permute-start(f32[6,1,96]{2,1,0:T(1,128)S(1)} %get-tuple-element.130), channel_id=1, source_target_pairs={{1,0},{2,1},{3,2},{4,3},{5,4},{6,5},{7,6},{8,7},{9,8},{10,9},{11,1... | collective-permute-start | bytes 6920 | tf_op jit(solution)/shard_map/ppermute | solution.py:20
  357.8 7.9 %collective-permute-start.50 = (f32[4,1,48]{2,1,0:T(1,128)S(1)}, f32[4,1,48]{2,1,0:T(1,128)S(1)}, u32[]{:S(2)}, u32[]{:S(2)}) collective-permute-start(f32[4,1,48]{2,1,0:T(1,128)S(1)} %get-tuple-element.183), channel_id=1, source_target_pairs={{0,1},{1,2},{2,3},{3,4},{4,5},{5,6},{6,7},{7,8},{8,9},{9,10},{10,1... | collective-permute-start | bytes 2312 | tf_op jit(solution)/shard_map/ppermute | solution.py:18
  (128 other events, 845.6 us)
where the time goes:
time: 795 us; the launch traced here: 783 us
  starting transfers between devices  408 us (51%)
  waiting for transfers between devices  201 us (25%)
  local copies, waits for them, and re-layouts  153 us (19%)
  other arithmetic  17.5 us (2%)
    ppermute x72, starting transfers between devices, extended(): lax.ppermute(tail, axis, [(i, (i + 1) % count) for i in range(ends)])  229 us
    ppermute x72, waiting for transfers between devices, extended(): lax.ppermute(head, axis, [((i + 1) % count, i) for i in range(ends)])  200 us
    ppermute x72, starting transfers between devices, extended(): lax.ppermute(head, axis, [((i + 1) % count, i) for i in range(ends)])  178 us
    unnamed x82, local copies, waits for them, and re-layouts  49.2 us
    another operation x6, local copies, waits for them, and re-layouts, blocks_of(): return field.reshape(sx // 2, 2, sy // 2, 2, sz // 2, 2)  48.2 us
    slice x12, local copies, waits for them, and re-layouts, face_average(): parts.append(block[:, first, :, second, :, third])  43 us
  transfers between devices with their start and end apart: 144, of which 58 were waited for; matrix products, arithmetic and copies ran while one was open for 21% of the time, Pallas kernels for 0%

commit v1 on v0

v1 whole, which is shorter than its diff:
```python
import functools

import numpy as np

import jax
import jax.numpy as jnp
from jax import lax
from jax.experimental import pallas as pl
from jax.experimental.pallas import tpu as pltpu
from jax.sharding import PartitionSpec as P

F32 = jnp.float32
MESH = pl.DeviceIdType.MESH
LANES = 128
BOTTOM = 8

_L, _D = np.float32(1.0), np.float32(0.1)
W_LL = float(np.float32(2) * _L * _L / (_L + _L))
W_MX = float(np.float32(2) * _L * _D / (_L + _D))
W_DD = float(np.float32(2) * _D * _D / (_D + _D))

REACH = 5
NEAR = [(dx, dy) for dx in (-1, 0, 1) for dy in (-1, 0, 1) if (dx, dy) != (0, 0)]
FAR = [(dx, dy) for dx in (-2, 2) for dy in (-1, 0, 1)]
WIDE = NEAR + FAR
ALONG = [d * s for d in range(1, REACH + 1) for s in (1, -1)]


def rot(v, shift):
    return pltpu.roll(v, shift, 1)


def span(step, own, size, take):
    if step == 0:
        return own, size
    if isinstance(take, tuple):
        take = take[0] if step < 0 else take[1]
    if step > 0:
        return own + size - take, take
    return own, take


def kernel(
    nx, ny,
    rs_hbm, ph_hbm, p_hbm, r_hbm,
    rs_in, ph_in, out_p, out_r,
    ph, rs, wf, sf, df, rdf, pf, pb0, rf, tf, f1o,
    f1, b1, wm, sm, dm, rdm, pm, mb0, rm, em,
    lw, lb, gw, gb, ul, wl, sl, rdl, plow, e1, xo_s,
    in_sem, out_sem,
    s_ph, r_ph, s_rs, r_rs, s_f1, r_f1, s_b1, r_b1, s_pb, r_pb, s_mb, r_mb,
    s_lw, r_lw, s_lb, r_lb, s_gw, r_gw, s_gb, r_gb,
):
    a = lax.axis_index("gx")
    b = lax.axis_index("gy")

    def exists(dx, dy):
        ok = None
        for pos, d, n in ((a, dx, nx), (b, dy, ny)):
            if d:
                one = (pos + d >= 0) if d < 0 else (pos + d < n)
                ok = one if ok is None else jnp.logical_and(ok, one)
        return ok

    started = []

    def copy(src, dst, ssem, rsem, i, dev):
        return pltpu.make_async_remote_copy(
            src_ref=src, dst_ref=dst, send_sem=ssem.at[i], recv_sem=rsem.at[i], device_id=dev, device_id_type=MESH
        )

    def send(steps, refs, ssem, rsem, base=0):
        for i, (dx, dy) in enumerate(steps):
            src, dst = refs(dx, dy)
            cp = functools.partial(copy, src, dst, ssem, rsem, base + i, (a + dx, b + dy))
            ok = exists(dx, dy)

            @pl.when(ok)
            def _():
                cp().start()

            started.append((ok, cp))

    def arrive(steps, refs, ssem, rsem, base=0):
        for i, (dx, dy) in enumerate(steps):
            src, dst = refs(dx, dy)

            @pl.when(exists(-dx, -dy))
            def _():
                copy(src, dst, ssem, rsem, base + i, (a - dx, b - dy)).wait_recv()

    def ring_send(src, dst, ssem, rsem):
        for d in range(1, nx):
            cp = functools.partial(copy, src, dst((4 - d) % nx), ssem, rsem, d - 1, (lax.rem(a + d, nx), b))
            cp().start()
            started.append((None, cp))

    def ring_arrive(src, dst, ssem, rsem):
        for d in range(1, nx):
            copy(src, dst((4 - d) % nx), ssem, rsem, d - 1, (lax.rem(a + nx - d, nx), b)).wait_recv()

    def fine_refs(arr, lead, pairs, rows):
        def refs(dx, dy):
            x0, xn = span(dx, 3, 4, pairs)
            y0, yn = span(dy, 8, 16, rows)
            pre = (slice(None),) * lead
            return (
                arr.at[pre + (pl.ds(x0, xn), slice(None), pl.ds(y0, yn))],
                arr.at[pre + (pl.ds(x0 - 4 * dx, xn), slice(None), pl.ds(y0 - 16 * dy, yn))],
            )

        return refs

    def mid_refs(arr, lead, own, size, far, rows):
        def refs(dx, dy):
            x0, xn = span(dx, own, size, size if abs(dx) < 2 else far)
            y0, yn = span(dy, 16, 8, rows)
            pre = (slice(None),) * lead
            return (
                arr.at[pre + (pl.ds(x0, xn), pl.ds(y0, yn))],
                arr.at[pre + (pl.ds(x0 - size * dx, xn), pl.ds(y0 - 8 * dy, yn))],
            )

        return refs

    def low_refs(arr, lead):
        def refs(dx, dy):
            pre = (slice(None),) * lead
            return arr.at[pre + (pl.ds(20, 4),)], arr.at[pre + (pl.ds(20 - 4 * dy, 4),)]

        return refs

    ph_refs = fine_refs(ph, 1, 3, 5)
    rs_refs = fine_refs(rs, 1, 2, 4)
    pb_refs = fine_refs(pb0, 0, 3, 5)
    f1_refs = mid_refs(f1, 1, 8, 4, (3, 2), (7, 6))
    b1_refs = mid_refs(b1, 0, 8, 4, 2, 6)
    mb_refs = mid_refs(mb0, 0, 4, 2, 2, 7)
    lw_refs = low_refs(lw, 1)
    lb_refs = low_refs(lb, 0)
    gy_steps = [(0, d) for d in ALONG]

    in_rs = pltpu.make_async_copy(rs_hbm, rs_in, in_sem.at[0])
    in_ph = pltpu.make_async_copy(ph_hbm, ph_in, in_sem.at[1])
    in_ph.start()
    in_rs.start()

    bar = pltpu.get_barrier_semaphore()
    greet = list(WIDE) + [(0, d) for d in ALONG if abs(d) > 1]
    count = jnp.int32(0)
    for dx, dy in greet:
        ok = exists(dx, dy)

        @pl.when(ok)
        def _():
            pl.semaphore_signal(bar, inc=1, device_id=(a + dx, b + dy), device_id_type=MESH)

        count = count + ok.astype(jnp.int32)
    for d in range(1, nx):
        t = lax.rem(a + d, nx)
        far = jnp.logical_or(t > a + 2, t < a - 2)

        @pl.when(far)
        def _():
            pl.semaphore_signal(bar, inc=1, device_id=(t, b), device_id_type=MESH)

        count = count + far.astype(jnp.int32)

    def iota(rows, dim):
        return lax.broadcasted_iota(jnp.int32, (rows, LANES), dim)

    def h1_of(rows):
        return iota(rows, 1) >= 64

    def lane_ok(rows):
        return lax.rem(iota(rows, 1), 64) < 48

    def odd_fine(rows, start, t):
        return lax.rem(iota(rows, 0) + (start + t), 2) == 1

    def odd_mid(rows, start):
        return lax.rem(iota(rows, 0) + start + lax.div(iota(rows, 1), 64), 2) == 1

    def odd_low(rows, start):
        return lax.rem(iota(rows, 0) + start + iota(rows, 1), 2) == 1

    def zero(ref):
        ref[...] = jnp.zeros(ref.shape, F32)

    @pl.when(a == 0)
    def _():
        zero(ph.at[:, 0:3]); zero(rs.at[:, 0:3]); zero(pb0.at[0:3]); zero(f1.at[:, 0:8]); zero(b1.at[0:8]); zero(mb0.at[0:4])

    @pl.when(a == 1)
    def _():
        zero(f1.at[:, 0:4]); zero(b1.at[0:4]); zero(mb0.at[0:2])

    @pl.when(a == nx - 1)
    def _():
        zero(ph.at[:, 7:10]); zero(rs.at[:, 7:10]); zero(pb0.at[7:10])
        zero(f1.at[:, 12:21]); zero(b1.at[12:20]); zero(mb0.at[6:10])

    @pl.when(a == nx - 2)
    def _():
        zero(f1.at[:, 16:21]); zero(b1.at[16:20]); zero(mb0.at[8:10])

    @pl.when(b == 0)
    def _():
        zero(ph.at[:, :, :, 0:8]); zero(rs.at[:, :, :, 0:8]); zero(pb0.at[:, :, 0:8])
        zero(f1.at[:, :, 0:16]); zero(b1.at[:, 0:16]); zero(mb0.at[:, 0:16])

    @pl.when(b == ny - 1)
    def _():
        zero(ph.at[:, :, :, 24:32]); zero(rs.at[:, :, :, 24:32]); zero(pb0.at[:, :, 24:32])
        zero(f1.at[:, :, 24:40]); zero(b1.at[:, 24:40]); zero(mb0.at[:, 24:40])

    for d in ALONG:
        @pl.when(jnp.logical_not(exists(0, d)))
        def _():
            zero(lw.at[:, pl.ds(20 + 4 * d, 4)])
            zero(lb.at[pl.ds(20 + 4 * d, 4)])

    nz = rs_in.shape[2]
    kk = lax.broadcasted_iota(jnp.int32, (nz, 2 * LANES), 0)
    cc = lax.broadcasted_iota(jnp.int32, (nz, 2 * LANES), 1)
    q, hh, tt = lax.rem(cc, 64), lax.rem(lax.div(cc, 64), 2), lax.div(cc, 128)
    perm = jnp.where(jnp.logical_and(kk == 4 * q + 2 * hh + tt, q < 48), 1.0, 0.0).astype(F32)

    def split_into(values, dst):
        for t in (0, 1):
            odd = odd_fine(16, 0, t)
            for m in range(4):
                lo = values[32 * m:32 * m + 16, t * LANES:(t + 1) * LANES]
                hi = values[32 * m + 16:32 * m + 32, t * LANES:(t + 1) * LANES]
                dst[0, 3 + m, t, 8:24, :] = jnp.where(odd, hi, lo)
                dst[1, 3 + m, t, 8:24, :] = jnp.where(odd, lo, hi)

    in_ph.wait()
    labels = jnp.where(ph_in[...] == 1, 1.0, 0.0).astype(F32).reshape(128, nz)
    split_into(jnp.dot(labels, perm, preferred_element_type=F32), ph)
    in_rs.wait()
    block = rs_in[...].reshape(128, nz)
    split_into(jnp.dot(block, perm, precision=lax.Precision.HIGHEST, preferred_element_type=F32), rs)

    pl.semaphore_wait(bar, count)
    send(NEAR, ph_refs, s_ph, r_ph)
    send(NEAR, rs_refs, s_rs, r_rs)

    def pair_ok(first, m, total):
        g = first + m
        return jnp.logical_and(g >= 0, g < total)

    def inside(rows, start, total, ok):
        g = iota(rows, 0) + (start + jnp.where(ok, 0, -4096))
        return jnp.logical_and(jnp.logical_and(g >= 0, g < total), lane_ok(rows))

    def fine_sides(arr, c, m, t, r0, n, odd, h1):
        o = 1 - c
        xs = arr[o, m, t, pl.ds(r0, n), :]
        lo = arr[o, m - 1, t, pl.ds(r0, n), :]
        hi = arr[o, m + 1, t, pl.ds(r0, n), :]
        xo = jnp.where(odd, hi, lo) if c == 0 else jnp.where(odd, lo, hi)
        ym = arr[o, m, t, pl.ds(r0 - 1, n), :]
        yp = arr[o, m, t, pl.ds(r0 + 1, n), :]
        zs = arr[o, m, 1 - t, pl.ds(r0, n), :]
        if t == 0:
            zo = jnp.where(h1, rot(zs, 64), rot(zs, 65))
        else:
            zo = jnp.where(h1, rot(zs, 63), rot(zs, 64))
        return xs, xo, ym, yp, zs, zo

    R0, RN = 4, 24
    odd24 = [odd_fine(RN, R0, 0), odd_fine(RN, R0, 1)]
    h24 = h1_of(RN)

    arrive(NEAR, ph_refs, s_ph, r_ph)

    def fine_weights(m, carry):
        valid = inside(RN, 16 * b - 8 + R0, 16 * ny, pair_ok(4 * a - 3, m, 4 * nx))
        fx = fy = fz = None
        for t in (0, 1):
            both = []
            for c in (0, 1):
                dense = ph[c, m, t, pl.ds(R0, RN), :] > 0.5
                on = jnp.where(dense, W_DD, W_MX)
                off = jnp.where(dense, W_MX, W_LL)
                w = [jnp.where(s > 0.5, on, off) for s in fine_sides(ph, c, m, t, R0, RN, odd24[t], h24)]
                dg = ((((w[0] + w[1]) + w[2]) + w[3]) + w[4]) + w[5]
                rd = jnp.where(valid, 1.0 / dg, 0.0)
                for f in range(6):
                    wf[6 * c + f, m, t, pl.ds(R0, RN), :] = w[f] * rd
                df[c, m, t, pl.ds(R0, RN), :] = dg
                rdf[c, m, t, pl.ds(R0, RN), :] = rd
                both.append(w)
            x = jnp.where(odd24[t], both[1][1], both[0][1])
            y = both[0][2] + both[1][2]
            fx = x if fx is None else fx + x
            fy = y if fy is None else fy + y
            if t == 0:
                fz = both[0][5] + both[1][5]
        tf[0, m, 0:RN, :] = fx
        tf[1, m, 0:RN, :] = fy
        tf[2, m, 0:RN, :] = fz
        return carry

    lax.fori_loop(1, 9, fine_weights, 0)

    even, oddr = pl.ds(0, 16, stride=2), pl.ds(1, 16, stride=2)

    def mid_faces(i, carry):
        f1o[0, i, 0:16, :] = 0.25 * (tf[0, i + 3, even, :] + tf[0, i + 3, oddr, :])
        f1o[1, i, 0:16, :] = 0.25 * tf[1, i + 3, even, :]
        f1o[2, i, 0:16, :] = 0.25 * (tf[2, i + 3, even, :] + tf[2, i + 3, oddr, :])
        return carry

    lax.fori_loop(0, 5, mid_faces, 0)
    h8 = h1_of(8)
    for i in range(4):
        fx, fxn = f1o[0, i, 2:10, :], f1o[0, i + 1, 2:10, :]
        fy, fyn = f1o[1, i, 2:10, :], f1o[1, i, 3:11, :]
        fz = f1o[2, i, 2:10, :]
        fzn = jnp.where(h8, rot(fz, 63), rot(fz, 64))
        f1[0, 8 + i, 16:24, :] = fx
        f1[1, 8 + i, 16:24, :] = fy
        f1[2, 8 + i, 16:24, :] = fz
        f1[3, 8 + i, 16:24, :] = ((((fx + fxn) + fy) + fyn) + fz) + fzn
    send(NEAR, f1_refs, s_f1, r_f1)

    def zsum(v):
        return v + rot(v, 64)

    fx2 = [0.25 * zsum(f1o[0, 2 * i, pl.ds(2, 8, stride=2), :] + f1o[0, 2 * i, pl.ds(3, 8, stride=2), :]) for i in range(3)]
    fy2, fy2n, fz2, fz2n = [], [], [], []
    for i in range(2):
        fy2.append(0.25 * zsum(f1o[1, 2 * i, pl.ds(2, 8, stride=2), :] + f1o[1, 2 * i + 1, pl.ds(2, 8, stride=2), :]))
        fy2n.append(0.25 * zsum(f1o[1, 2 * i, pl.ds(4, 8, stride=2), :] + f1o[1, 2 * i + 1, pl.ds(4, 8, stride=2), :]))
        v = (f1o[2, 2 * i, pl.ds(2, 8, stride=2), :] + f1o[2, 2 * i, pl.ds(3, 8, stride=2), :]) + (
            f1o[2, 2 * i + 1, pl.ds(2, 8, stride=2), :] + f1o[2, 2 * i + 1, pl.ds(3, 8, stride=2), :]
        )
        v = 0.25 * jnp.where(h8, rot(v, 64), v)
        fz2.append(v)
        fz2n.append(rot(v, 127))
    odd8 = odd_low(8, 0)
    dg2 = [((((fx2[i] + fx2[i + 1]) + fy2[i]) + fy2n[i]) + fz2[i]) + fz2n[i] for i in range(2)]
    rd2 = [jnp.where(lane_ok(8), 1.0 / d, 0.0) for d in dg2]

    def red(v):
        return jnp.where(odd8, v[1], v[0])

    def black(v):
        return jnp.where(odd8, v[0], v[1])

    edge_low = jnp.where(a == 0, 0.0, 1.0)
    edge_high = jnp.where(a == nx - 1, 0.0, 1.0)
    xo2 = jnp.where(odd8, fx2[2] * edge_high, fx2[0] * edge_low)
    for f, (first, second) in enumerate(
        ((fx2[1], xo2), (red(fy2), red(fy2n)), (red(fz2), red(fz2n)), (red(rd2), black(rd2)))
    ):
        lw[f, 20:24, :] = jnp.where(h8, second, first)[0:4]
    send(gy_steps, lw_refs, s_lw, r_lw)

    def fine_nb(c, m, t, r0, n, odd, h1):
        v = fine_sides(pf, c, m, t, r0, n, odd, h1)
        total = wf[6 * c, m, t, pl.ds(r0, n), :] * v[0]
        for f in range(1, 6):
            total = total + wf[6 * c + f, m, t, pl.ds(r0, n), :] * v[f]
        return total

    def fine_half(c, m0, m1, r0, n):
        odd = [odd_fine(n, r0, 0), odd_fine(n, r0, 1)]
        h1 = h1_of(n)

        def body(m, carry):
            for t in (0, 1):
                nb = fine_nb(c, m, t, r0, n, odd[t], h1)
                pf[c, m, t, pl.ds(r0, n), :] = sf[c, m, t, pl.ds(r0, n), :] + nb
            return carry

        lax.fori_loop(m0, m1, body, 0)

    def fine_last(r0, n):
        odd = [odd_fine(n, r0, 0), odd_fine(n, r0, 1)]
        h1 = h1_of(n)

        def body(m, carry):
            for t in (0, 1):
                win = pl.ds(r0, n)
                nb = fine_nb(1, m, t, r0, n, odd[t], h1)
                fresh = sf[1, m, t, win, :] + nb
                pf[1, m, t, win, :] = fresh
                rf[1, m, t, win, :] = rs[1, m, t, win, :] - df[1, m, t, win, :] * (fresh - nb)
            return carry

        lax.fori_loop(2, 8, body, 0)

    def fine_red_residual():
        odd = [odd_fine(16, 8, 0), odd_fine(16, 8, 1)]
        h1 = h1_of(16)

        def body(m, carry):
            for t in (0, 1):
                win = pl.ds(8, 16)
                nb = fine_nb(0, m, t, 8, 16, odd[t], h1)
                rf[0, m, t, win, :] = rs[0, m, t, win, :] - df[0, m, t, win, :] * (pf[0, m, t, win, :] - nb)
            return carry

        lax.fori_loop(3, 7, body, 0)

    arrive(NEAR, rs_refs, s_rs, r_rs)

    def fine_source(m, carry):
        win = pl.ds(R0, RN)
        for t in (0, 1):
            first = rs[0, m, t, win, :] * rdf[0, m, t, win, :]
            sf[0, m, t, win, :] = first
            pf[0, m, t, win, :] = first
            sf[1, m, t, win, :] = rs[1, m, t, win, :] * rdf[1, m, t, win, :]
        return carry

    lax.fori_loop(1, 9, fine_source, 0)
    fine_half(1, 1, 9, 4, 24)
    fine_half(0, 2, 8, 6, 24)
    fine_last(7, 24)
    fine_red_residual()

    def restrict_fine(m, carry):
        v = (rf[0, m, 0, 8:24, :] + rf[1, m, 0, 8:24, :]) + (rf[0, m, 1, 8:24, :] + rf[1, m, 1, 8:24, :])
        rm[m, 0:16, :] = v
        b1[m + 5, 16:24, :] = 0.125 * (rm[m, pl.ds(0, 8, stride=2), :] + rm[m, pl.ds(1, 8, stride=2), :])
        return carry

    lax.fori_loop(3, 7, restrict_fine, 0)
    send(WIDE, b1_refs, s_b1, r_b1)

    def keep_black(m, carry):
        for t in (0, 1):
            pb0[m, t, 8:24, :] = pf[1, m, t, 8:24, :]
        return carry

    lax.fori_loop(3, 7, keep_black, 0)
    send(NEAR, pb_refs, s_pb, r_pb)
    send(FAR, f1_refs, s_f1, r_f1, len(NEAR))

    def mid_weights(m0, m1, r0, n, top):
        odd, h1 = odd_mid(n, r0), h1_of(n)
        win, nxt = pl.ds(r0, n), pl.ds(r0 + 1, n)

        def body(m, carry):
            valid = inside(n, 8 * b - 16 + r0, 8 * ny, pair_ok(2 * a - 4, m, 2 * nx))
            e0, e1_ = 2 * m, 2 * m + 1
            fx0, fx1, fx2_ = f1[0, e0, win, :], f1[0, e1_, win, :], f1[0, jnp.minimum(e1_ + 1, top), win, :]
            ym = [f1[1, e, win, :] for e in (e0, e1_)]
            yp = [f1[1, e, nxt, :] for e in (e0, e1_)]
            fz = [f1[2, e, win, :] for e in (e0, e1_)]
            zs = [jnp.where(h1, v, rot(v, 64)) for v in fz]
            zo = [jnp.where(h1, rot(v, 63), v) for v in fz]
            dg = [f1[3, e, win, :] for e in (e0, e1_)]
            for c in (0, 1):
                def pick(v):
                    return jnp.where(odd, v[1 - c], v[c])

                xo = jnp.where(odd, fx2_, fx0) if c == 0 else jnp.where(odd, fx0, fx2_)
                d = pick(dg)
                rd = jnp.where(valid, 1.0 / d, 0.0)
                for f, w in enumerate((fx1, xo, pick(ym), pick(yp), pick(zs), pick(zo))):
                    wm[6 * c + f, m, win, :] = w * rd
                dm[c, m, win, :] = d
                rdm[c, m, win, :] = rd
            return carry

        lax.fori_loop(m0, m1, body, 0)

    def mid_source(m0, m1, r0, n, start):
        odd = odd_mid(n, r0)
        win = pl.ds(r0, n)

        def body(m, carry):
            lo, hi = b1[2 * m, win, :], b1[2 * m + 1, win, :]
            first = 4.0 * jnp.where(odd, hi, lo) * rdm[0, m, win, :]
            sm[0, m, win, :] = first
            if start:
                pm[0, m, win, :] = first
            sm[1, m, win, :] = 4.0 * jnp.where(odd, lo, hi) * rdm[1, m, win, :]
            return carry

        lax.fori_loop(m0, m1, body, 0)

    def mid_nb(c, m, r0, n, odd, h1):
        o = 1 - c
        win = pl.ds(r0, n)
        xs, lo, hi = pm[o, m, win, :], pm[o, m - 1, win, :], pm[o, m + 1, win, :]
        xo = jnp.where(odd, hi, lo) if c == 0 else jnp.where(odd, lo, hi)
        zo = jnp.where(h1, rot(xs, 63), rot(xs, 65))
        total = wm[6 * c, m, win, :] * xs
        total = total + wm[6 * c + 1, m, win, :] * xo
        total = total + wm[6 * c + 2, m, win, :] * pm[o, m, pl.ds(r0 - 1, n), :]
        total = total + wm[6 * c + 3, m, win, :] * pm[o, m, pl.ds(r0 + 1, n), :]
        total = total + wm[6 * c + 4, m, win, :] * rot(xs, 64)
        return total + wm[6 * c + 5, m, win, :] * zo

    def mid_half(c, m0, m1, r0, n):
        odd, h1 = odd_mid(n, r0), h1_of(n)

        def body(m, carry):
            win = pl.ds(r0, n)
            pm[c, m, win, :] = sm[c, m, win, :] + mid_nb(c, m, r0, n, odd, h1)
            return carry

        lax.fori_loop(m0, m1, body, 0)

    arrive(NEAR, f1_refs, s_f1, r_f1)
    mid_weights(2, 8, 12, 16, 15)
    arrive(gy_steps, lw_refs, s_lw, r_lw)
    ring_send(lw.at[:, 0:44], lambda i: gw.at[i, :, 0:44], s_gw, r_gw)
    arrive(NEAR, b1_refs, s_b1, r_b1)
    mid_source(2, 8, 12, 16, True)
    mid_half(1, 2, 8, 13, 16)
    mid_half(0, 3, 7, 14, 16)
    mid_half(1, 3, 7, 15, 16)

    odd_own, h_own = odd_mid(8, 16), h1_of(8)
    own = pl.ds(16, 8)
    planes = []
    for m in (4, 5):
        lo, hi = b1[2 * m, own, :], b1[2 * m + 1, own, :]
        total = None
        for c in (0, 1):
            src = jnp.where(odd_own, hi, lo) if c == 0 else jnp.where(odd_own, lo, hi)
            nb = mid_nb(c, m, 16, 8, odd_own, h_own)
            res = src - dm[c, m, own, :] * (pm[c, m, own, :] - nb) * 0.25
            total = res if total is None else total + res
        rm[m, 0:8, :] = total
        rm[m, 8:16, :] = total
        planes.append(0.125 * zsum(rm[m, pl.ds(0, 8, stride=2), :] + rm[m, pl.ds(1, 8, stride=2), :]))
    lb[20:24, :] = jnp.where(h8, black(planes), red(planes))[0:4]
    send(gy_steps, lb_refs, s_lb, r_lb)
    for m in (4, 5):
        mb0[m, own, :] = pm[1, m, own, :]
    send(WIDE, mb_refs, s_mb, r_mb)

    arrive(FAR, f1_refs, s_f1, r_f1, len(NEAR))
    mid_weights(1, 9, 8, 24, 18)
    arrive(FAR, b1_refs, s_b1, r_b1, len(NEAR))
    mid_source(1, 9, 8, 24, False)

    arrive(gy_steps, lb_refs, s_lb, r_lb)
    ring_send(lb.at[0:44], lambda i: gb.at[i, 0:44], s_gb, r_gb)
    gw[4, :, 0:44] = lw[:, 0:44]
    gb[4, 0:44] = lb[0:44]

    LR = 48
    h48 = h1_of(LR)
    odd48 = odd_low(LR, 0)
    lwin = pl.ds(8, LR)

    def fold(lo, hi, half):
        if half == 0:
            return jnp.where(h48, rot(hi, 64), lo)
        return jnp.where(h48, hi, rot(lo, 64))

    ring_arrive(lw.at[:, 0:44], lambda i: gw.at[i, :, 0:44], s_gw, r_gw)

    def low_weights(s, carry):
        rdl[0, s, lwin, :] = fold(gw[s, 3], gw[s + 8, 3], 0)
        rdl[1, s, lwin, :] = fold(gw[s, 3], gw[s + 8, 3], 1)
        rd = rdl[0, s, lwin, :]
        for f in range(6):
            u = fold(gw[s, f // 2], gw[s + 8, f // 2], f % 2)
            ul[f, s + 1, lwin, :] = u
            wl[f, s, lwin, :] = u * rd
        return carry

    lax.fori_loop(0, 8, low_weights, 0)
    ul[1, 0, lwin, :] = rot(ul[1, 8, lwin, :], 64)
    ul[1, 9, lwin, :] = rot(ul[1, 1, lwin, :], 64)

    def low_black(s, carry):
        rd = rdl[1, s, lwin, :]
        wl[6, s, lwin, :] = ul[0, s + 1, lwin, :] * rd
        wl[7, s, lwin, :] = jnp.where(odd48, ul[1, s, lwin, :], ul[1, s + 2, lwin, :]) * rd
        wl[8, s, lwin, :] = ul[3, s + 1, pl.ds(7, LR), :] * rd
        wl[9, s, lwin, :] = ul[2, s + 1, pl.ds(9, LR), :] * rd
        wl[10, s, lwin, :] = rot(ul[5, s + 1, lwin, :], 1) * rd
        wl[11, s, lwin, :] = rot(ul[4, s + 1, lwin, :], 127) * rd
        return carry

    lax.fori_loop(0, 8, low_black, 0)

    ring_arrive(lb.at[0:44], lambda i: gb.at[i, 0:44], s_gb, r_gb)

    def low_source(s, carry):
        lo, hi = gb[s], gb[s + 8]
        first = 16.0 * fold(lo, hi, 0) * rdl[0, s, lwin, :]
        sl[0, s, lwin, :] = first
        plow[0, s + 1, lwin, :] = first
        sl[1, s, lwin, :] = 16.0 * fold(lo, hi, 1) * rdl[1, s, lwin, :]
        return carry

    lax.fori_loop(0, 8, low_source, 0)

    def low_ghosts(c, r0, n):
        win = pl.ds(r0, n)
        plow[c, 0, win, :] = rot(plow[c, 8, win, :], 64)
        plow[c, 9, win, :] = rot(plow[c, 1, win, :], 64)

    low_ghosts(0, 8, LR)
    for half in range(2, 2 * BOTTOM + 1):
        c = (half - 1) % 2
        reach = 4 + 2 * BOTTOM - half
        r0, n = 8 + 20 - reach, 8 * ((4 + 2 * reach + 7) // 8)
        odd = odd_low(n, r0)

        def low_body(s, carry, c=c, r0=r0, n=n, odd=odd):
            o = 1 - c
            win = pl.ds(r0, n)
            xs, lo, hi = plow[o, s + 1, win, :], plow[o, s, win, :], plow[o, s + 2, win, :]
            xo = jnp.where(odd, hi, lo) if c == 0 else jnp.where(odd, lo, hi)
            total = sl[c, s, win, :] + wl[6 * c, s, win, :] * xs
            total = total + wl[6 * c + 1, s, win, :] * xo
            total = total + wl[6 * c + 2, s, win, :] * plow[o, s + 1, pl.ds(r0 - 1, n), :]
            total = total + wl[6 * c + 3, s, win, :] * plow[o, s + 1, pl.ds(r0 + 1, n), :]
            total = total + wl[6 * c + 4, s, win, :] * rot(xs, 1)
            plow[c, s + 1, win, :] = total + wl[6 * c + 5, s, win, :] * rot(xs, 127)
            return carry

        lax.fori_loop(0, 8, low_body, 0)
        low_ghosts(c, r0, n)

    arrive(WIDE, mb_refs, s_mb, r_mb)
    odd16, h16 = odd_low(16, 0), h1_of(16)
    rows24 = pl.ds(8, 24)

    def mid_correct(s, carry):
        red_, black_ = plow[0, s + 3, pl.ds(24, 16), :], plow[1, s + 3, pl.ds(24, 16), :]
        for e in (0, 1):
            v = jnp.where(odd16, black_, red_) if e == 0 else jnp.where(odd16, red_, black_)
            v = jnp.where(h16, rot(v, 64), v)
            em[2 * s + e, pl.ds(0, 16, stride=2), :] = v
            em[2 * s + e, pl.ds(1, 16, stride=2), :] = v
            m = 2 * s + e
            add = em[m, 0:24, :] * jnp.where(pair_ok(2 * a - 4, m, 2 * nx), 1.0, 0.0)
            pm[1, m, rows24, :] = mb0[m, rows24, :] + add
        return carry

    lax.fori_loop(0, 5, mid_correct, 0)
    mid_half(0, 1, 9, 10, 24)
    mid_half(1, 1, 9, 11, 24)
    mid_half(0, 2, 8, 12, 16)
    mid_half(1, 2, 8, 13, 16)

    arrive(NEAR, pb_refs, s_pb, r_pb)
    odd_c = odd_mid(16, 13)

    for m in range(10):
        n, e = (m + 5) // 2, (m + 5) % 2
        red_, black_ = pm[0, n, pl.ds(13, 16), :], pm[1, n, pl.ds(13, 16), :]
        v = jnp.where(odd_c, black_, red_) if e == 0 else jnp.where(odd_c, red_, black_)
        e1[m, pl.ds(2, 16, stride=2), :] = v
        e1[m, pl.ds(3, 16, stride=2), :] = v
        for t in (0, 1):
            pf[1, m, t, pl.ds(3, 32), :] = pb0[m, t, pl.ds(3, 32), :] + e1[m, pl.ds(3, 32), :]

    fine_half(0, 1, 9, 4, 24)
    fine_half(1, 1, 9, 5, 24)
    fine_half(0, 2, 8, 6, 24)
    fine_last(7, 24)
    fine_red_residual()

    kk2 = lax.broadcasted_iota(jnp.int32, (2 * LANES, nz), 1)
    cc2 = lax.broadcasted_iota(jnp.int32, (2 * LANES, nz), 0)
    q2, hh2, tt2 = lax.rem(cc2, 64), lax.rem(lax.div(cc2, 64), 2), lax.div(cc2, 128)
    back = jnp.where(jnp.logical_and(kk2 == 4 * q2 + 2 * hh2 + tt2, q2 < 48), 1.0, 0.0).astype(F32)

    def join_from(src, out):
        for t in (0, 1):
            odd = odd_fine(16, 8, t)
            for m in range(4):
                r, k = src[0, 3 + m, t, 8:24, :], src[1, 3 + m, t, 8:24, :]
                xo_s[32 * m:32 * m + 16, t * LANES:(t + 1) * LANES] = jnp.where(odd, k, r)
                xo_s[32 * m + 16:32 * m + 32, t * LANES:(t + 1) * LANES] = jnp.where(odd, r, k)
        v = jnp.dot(xo_s[...], back, precision=lax.Precision.HIGHEST, preferred_element_type=F32)
        out[...] = v.reshape(out.shape)

    join_from(pf, out_p)
    put_p = pltpu.make_async_copy(out_p, p_hbm, out_sem.at[0])
    put_p.start()
    join_from(rf, out_r)
    put_r = pltpu.make_async_copy(out_r, r_hbm, out_sem.at[1])
    put_r.start()
    for ok, cp in started:
        if ok is None:
            cp().wait_send()
        else:
            @pl.when(ok)
            def _():
                cp().wait_send()
    put_p.wait()
    put_r.wait()


def solution(mesh):
    nx, ny = mesh.shape["gx"], mesh.shape["gy"]

    def local(right_side, phase):
        shape = right_side.shape
        v = lambda *dims: pltpu.VMEM(dims, F32)
        sems = []
        for n in (len(NEAR), len(NEAR), len(WIDE), len(WIDE), len(NEAR), len(WIDE), len(ALONG), len(ALONG), nx - 1, nx - 1):
            sems += [pltpu.SemaphoreType.DMA((n,)), pltpu.SemaphoreType.DMA((n,))]
        fine = (10, 2, 40, LANES)
        return pl.pallas_call(
            functools.partial(kernel, nx, ny),
            out_shape=[jax.ShapeDtypeStruct(shape, F32)] * 2,
            in_specs=[pl.BlockSpec(memory_space=pl.ANY)] * 2,
            out_specs=[pl.BlockSpec(memory_space=pl.ANY)] * 2,
            scratch_shapes=[
                v(*shape), pltpu.VMEM(shape, jnp.int32), v(*shape), v(*shape),
                v(2, *fine), v(2, *fine), v(12, *fine), v(2, *fine), v(2, *fine), v(2, *fine), v(2, *fine), v(*fine),
                v(2, *fine), v(3, 10, 32, LANES), v(3, 5, 24, LANES),
                v(4, 21, 40, LANES), v(20, 40, LANES), v(12, 10, 40, LANES), v(2, 10, 40, LANES), v(2, 10, 40, LANES),
                v(2, 10, 40, LANES), v(2, 10, 40, LANES), v(10, 40, LANES), v(10, 16, LANES), v(10, 32, LANES),
                v(4, 48, LANES), v(48, LANES), v(16, 4, 48, LANES), v(16, 48, LANES), v(6, 10, 64, LANES),
                v(12, 8, 64, LANES), v(2, 8, 64, LANES), v(2, 8, 64, LANES), v(2, 10, 64, LANES), v(10, 40, LANES),
                v(128, 2 * LANES),
                pltpu.SemaphoreType.DMA((2,)), pltpu.SemaphoreType.DMA((2,)),
            ] + sems,
            compiler_params=pltpu.CompilerParams(
                collective_id=0, has_side_effects=True, vmem_limit_bytes=48 * 2**20
            ),
        )(right_side, phase)

    spec = P("gx", "gy", None)
    return jax.shard_map(local, mesh=mesh, in_specs=(spec, spec), out_specs=(spec, spec), check_vma=False)
```

time: 795 us -> 80.7 us (0.10)
  the two profiles are of different devices: /device:TPU:103 before, /device:TPU:65 now
where the time goes in v1:
time: 80.7 us; the launch traced here: 80.6 us
  Pallas kernels  76.8 us (95%)
  local copies, waits for them, and re-layouts  3.11 us (4%)
    pallas_call x1, Pallas kernels, local(): pl.pallas_call(functools.partial(kernel, nx, ny), out_shape=[jax.ShapeDty...  76.8 us
    unnamed x6, local copies, waits for them, and re-layouts  3.11 us

profile of v1, /device:TPU:65, one launch (start us, length us, event | category | flops | bytes accessed | tf_op | source)
XLA Modules:
  0.0 80.6 jit_solution(10625719301122443500)
XLA Ops:
  0.6 0.0 copy-start
  0.6 0.9 %copy-done = f32[8,16,192]{2,1,0:T(8,128)S(1)} copy-done((f32[8,16,192]{2,1,0:T(8,128)S(1)}, f32[8,16,192]{2,1,0:T(8,128)}, u32[]{:S(2)}) %copy-start) | copy-done | bytes 98328
  1.5 0.0 copy-start.1
  1.5 0.9 %copy-done.1 = s32[8,16,192]{2,1,0:T(8,128)S(1)} copy-done((s32[8,16,192]{2,1,0:T(8,128)S(1)}, s32[8,16,192]{2,1,0:T(8,128)}, u32[]{:S(2)}) %copy-start.1) | copy-done | bytes 98328
  2.4 76.8 %shard_map.41 = (f32[8,16,192]{2,1,0:T(8,128)S(1)}, f32[8,16,192]{2,1,0:T(8,128)S(1)}) custom-call(f32[8,16,192]{2,1,0:T(8,128)S(1)} %copy-done, s32[8,16,192]{2,1,0:T(8,128)S(1)} %copy-done.1), custom_call_target="tpu_custom_call" | custom-call | tf_op jit(solution)/shard_map/pallas_call | solution.py:711
  79.3 0.7 copy.6
  79.9 0.7 copy.7
Async XLA Ops:
  0.6 0.9 %copy-start = (f32[8,16,192]{2,1,0:T(8,128)S(1)}, f32[8,16,192]{2,1,0:T(8,128)}, u32[]{:S(2)}) copy-start(f32[8,16,192]{2,1,0:T(8,128)} %rs_hbm.1) | copy-start | bytes 294916
  1.5 0.9 %copy-start.1 = (s32[8,16,192]{2,1,0:T(8,128)S(1)}, s32[8,16,192]{2,1,0:T(8,128)}, u32[]{:S(2)}) copy-start(s32[8,16,192]{2,1,0:T(8,128)} %ph_hbm.1) | copy-start | bytes 294916

commit v2 on v1

--- a/solution.py
+++ b/solution.py
@@ -49,7 +49,7 @@
     lw, lb, gw, gb, ul, wl, sl, rdl, plow, e1, xo_s,
     in_sem, out_sem,
     s_ph, r_ph, s_rs, r_rs, s_f1, r_f1, s_b1, r_b1, s_pb, r_pb, s_mb, r_mb,
-    s_lw, r_lw, s_lb, r_lb, s_gw, r_gw, s_gb, r_gb,
+    s_lw, r_lw, s_lb, r_lb, s_gw, r_gw, s_gb, r_gb, s_re, r_re,
 ):
     a = lax.axis_index("gx")
     b = lax.axis_index("gy")
@@ -94,6 +94,21 @@
             cp = functools.partial(copy, src, dst((4 - d) % nx), ssem, rsem, d - 1, (lax.rem(a + d, nx), b))
             cp().start()
             started.append((None, cp))
+
+    def relay_refs(i):
+        core = lax.rem(b, 2)
+        return gw.at[i, :, pl.ds(4 + 16 * core, 20)], gw.at[i, :, pl.ds(24 * core, 20)], (a, b + 1 - 2 * core)
+
+    def relay(i):
+        src, dst, dev = relay_refs(i)
+        cp = functools.partial(copy, src, dst, s_re, r_re, i, dev)
+        cp().start()
+        started.append((None, cp))
+
+    def relay_arrive(i):
+        src, dst, dev = relay_refs(i)
+        core = lax.rem(b, 2)
+        copy(src, gw.at[i, :, pl.ds(24 - 24 * core, 20)], s_re, r_re, i, dev).wait_recv()
 
     def ring_arrive(src, dst, ssem, rsem):
         for d in range(1, nx):
@@ -313,7 +328,7 @@
         f1o[2, i, 0:16, :] = 0.25 * (tf[2, i + 3, even, :] + tf[2, i + 3, oddr, :])
         return carry
 
-    lax.fori_loop(0, 5, mid_faces, 0)
+    lax.fori_loop(0, 5, mid_faces, 0, unroll=True)
     h8 = h1_of(8)
     for i in range(4):
         fx, fxn = f1o[0, i, 2:10, :], f1o[0, i + 1, 2:10, :]
@@ -353,10 +368,10 @@
     edge_low = jnp.where(a == 0, 0.0, 1.0)
     edge_high = jnp.where(a == nx - 1, 0.0, 1.0)
     xo2 = jnp.where(odd8, fx2[2] * edge_high, fx2[0] * edge_low)
-    for f, (first, second) in enumerate(
-        ((fx2[1], xo2), (red(fy2), red(fy2n)), (red(fz2), red(fz2n)), (red(rd2), black(rd2)))
-    ):
-        lw[f, 20:24, :] = jnp.where(h8, second, first)[0:4]
+    inv = jnp.where(h8, black(rd2), red(rd2))
+    for f, (first, second) in enumerate(((fx2[1], xo2), (red(fy2), red(fy2n)), (red(fz2), red(fz2n)))):
+        v = jnp.where(lane_ok(8), jnp.where(h8, second, first), rot(inv, 48 - 16 * f))
+        lw[f, 20:24, :] = v[0:4]
     send(gy_steps, lw_refs, s_lw, r_lw)
 
     def fine_nb(c, m, t, r0, n, odd, h1):
@@ -376,7 +391,7 @@
                 pf[c, m, t, pl.ds(r0, n), :] = sf[c, m, t, pl.ds(r0, n), :] + nb
             return carry
 
-        lax.fori_loop(m0, m1, body, 0)
+        lax.fori_loop(m0, m1, body, 0, unroll=True)
 
     def fine_last(r0, n):
         odd = [odd_fine(n, r0, 0), odd_fine(n, r0, 1)]
@@ -391,7 +406,7 @@
                 rf[1, m, t, win, :] = rs[1, m, t, win, :] - df[1, m, t, win, :] * (fresh - nb)
             return carry
 
-        lax.fori_loop(2, 8, body, 0)
+        lax.fori_loop(2, 8, body, 0, unroll=True)
 
     def fine_red_residual():
         odd = [odd_fine(16, 8, 0), odd_fine(16, 8, 1)]
@@ -404,7 +419,7 @@
                 rf[0, m, t, win, :] = rs[0, m, t, win, :] - df[0, m, t, win, :] * (pf[0, m, t, win, :] - nb)
             return carry
 
-        lax.fori_loop(3, 7, body, 0)
+        lax.fori_loop(3, 7, body, 0, unroll=True)
 
     arrive(NEAR, rs_refs, s_rs, r_rs)
 
@@ -417,7 +432,7 @@
             sf[1, m, t, win, :] = rs[1, m, t, win, :] * rdf[1, m, t, win, :]
         return carry
 
-    lax.fori_loop(1, 9, fine_source, 0)
+    lax.fori_loop(1, 9, fine_source, 0, unroll=True)
     fine_half(1, 1, 9, 4, 24)
     fine_half(0, 2, 8, 6, 24)
     fine_last(7, 24)
@@ -429,7 +444,7 @@
         b1[m + 5, 16:24, :] = 0.125 * (rm[m, pl.ds(0, 8, stride=2), :] + rm[m, pl.ds(1, 8, stride=2), :])
         return carry
 
-    lax.fori_loop(3, 7, restrict_fine, 0)
+    lax.fori_loop(3, 7, restrict_fine, 0, unroll=True)
     send(WIDE, b1_refs, s_b1, r_b1)
 
     def keep_black(m, carry):
@@ -437,7 +452,7 @@
             pb0[m, t, 8:24, :] = pf[1, m, t, 8:24, :]
         return carry
 
-    lax.fori_loop(3, 7, keep_black, 0)
+    lax.fori_loop(3, 7, keep_black, 0, unroll=True)
     send(NEAR, pb_refs, s_pb, r_pb)
     send(FAR, f1_refs, s_f1, r_f1, len(NEAR))
 
@@ -468,7 +483,7 @@
                 rdm[c, m, win, :] = rd
             return carry
 
-        lax.fori_loop(m0, m1, body, 0)
+        lax.fori_loop(m0, m1, body, 0, unroll=True)
 
     def mid_source(m0, m1, r0, n, start):
         odd = odd_mid(n, r0)
@@ -483,7 +498,7 @@
             sm[1, m, win, :] = 4.0 * jnp.where(odd, lo, hi) * rdm[1, m, win, :]
             return carry
 
-        lax.fori_loop(m0, m1, body, 0)
+        lax.fori_loop(m0, m1, body, 0, unroll=True)
 
     def mid_nb(c, m, r0, n, odd, h1):
         o = 1 - c
@@ -506,12 +521,13 @@
             pm[c, m, win, :] = sm[c, m, win, :] + mid_nb(c, m, r0, n, odd, h1)
             return carry
 
-        lax.fori_loop(m0, m1, body, 0)
+        lax.fori_loop(m0, m1, body, 0, unroll=True)
 
     arrive(NEAR, f1_refs, s_f1, r_f1)
     mid_weights(2, 8, 12, 16, 15)
     arrive(gy_steps, lw_refs, s_lw, r_lw)
-    ring_send(lw.at[:, 0:44], lambda i: gw.at[i, :, 0:44], s_gw, r_gw)
+    half_rows = pl.ds(20 * lax.rem(b, 2), 24)
+    ring_send(lw.at[:, half_rows], lambda i: gw.at[i, :, half_rows], s_gw, r_gw)
     arrive(NEAR, b1_refs, s_b1, r_b1)
     mid_source(2, 8, 12, 16, True)
     mid_half(1, 2, 8, 13, 16)
@@ -551,6 +567,7 @@
     LR = 48
     h48 = h1_of(LR)
     odd48 = odd_low(LR, 0)
+    q48 = lax.rem(iota(LR, 1), 64)
     lwin = pl.ds(8, LR)
 
     def fold(lo, hi, half):
@@ -558,19 +575,26 @@
             return jnp.where(h48, rot(hi, 64), lo)
         return jnp.where(h48, hi, rot(lo, 64))
 
-    ring_arrive(lw.at[:, 0:44], lambda i: gw.at[i, :, 0:44], s_gw, r_gw)
+    ring_arrive(lw.at[:, half_rows], lambda i: gw.at[i, :, half_rows], s_gw, r_gw)
+    for i in range(nx):
+        if i != 4:
+            relay(i)
+    for i in range(nx):
+        if i != 4:
+            relay_arrive(i)
 
     def low_weights(s, carry):
-        rdl[0, s, lwin, :] = fold(gw[s, 3], gw[s + 8, 3], 0)
-        rdl[1, s, lwin, :] = fold(gw[s, 3], gw[s + 8, 3], 1)
+        u = [fold(gw[s, f // 2], gw[s + 8, f // 2], f % 2) for f in range(6)]
+        for c in (0, 1):
+            third = jnp.where(q48 < 16, rot(u[c], 80), jnp.where(q48 < 32, rot(u[2 + c], 96), rot(u[4 + c], 112)))
+            rdl[c, s, lwin, :] = jnp.where(q48 < 48, third, 0.0)
         rd = rdl[0, s, lwin, :]
         for f in range(6):
-            u = fold(gw[s, f // 2], gw[s + 8, f // 2], f % 2)
-            ul[f, s + 1, lwin, :] = u
-            wl[f, s, lwin, :] = u * rd
-        return carry
-
-    lax.fori_loop(0, 8, low_weights, 0)
+            ul[f, s + 1, lwin, :] = u[f]
+            wl[f, s, lwin, :] = u[f] * rd
+        return carry
+
+    lax.fori_loop(0, 8, low_weights, 0, unroll=True)
     ul[1, 0, lwin, :] = rot(ul[1, 8, lwin, :], 64)
     ul[1, 9, lwin, :] = rot(ul[1, 1, lwin, :], 64)
 
@@ -584,7 +608,7 @@
         wl[11, s, lwin, :] = rot(ul[4, s + 1, lwin, :], 127) * rd
         return carry
 
-    lax.fori_loop(0, 8, low_black, 0)
+    lax.fori_loop(0, 8, low_black, 0, unroll=True)
 
     ring_arrive(lb.at[0:44], lambda i: gb.at[i, 0:44], s_gb, r_gb)
 
@@ -596,7 +620,7 @@
         sl[1, s, lwin, :] = 16.0 * fold(lo, hi, 1) * rdl[1, s, lwin, :]
         return carry
 
-    lax.fori_loop(0, 8, low_source, 0)
+    lax.fori_loop(0, 8, low_source, 0, unroll=True)
 
     def low_ghosts(c, r0, n):
         win = pl.ds(r0, n)
@@ -623,7 +647,7 @@
             plow[c, s + 1, win, :] = total + wl[6 * c + 5, s, win, :] * rot(xs, 127)
             return carry
 
-        lax.fori_loop(0, 8, low_body, 0)
+        lax.fori_loop(0, 8, low_body, 0, unroll=True)
         low_ghosts(c, r0, n)
 
     arrive(WIDE, mb_refs, s_mb, r_mb)
@@ -642,7 +666,7 @@
             pm[1, m, rows24, :] = mb0[m, rows24, :] + add
         return carry
 
-    lax.fori_loop(0, 5, mid_correct, 0)
+    lax.fori_loop(0, 5, mid_correct, 0, unroll=True)
     mid_half(0, 1, 9, 10, 24)
     mid_half(1, 1, 9, 11, 24)
     mid_half(0, 2, 8, 12, 16)
@@ -705,7 +729,7 @@
         shape = right_side.shape
         v = lambda *dims: pltpu.VMEM(dims, F32)
         sems = []
-        for n in (len(NEAR), len(NEAR), len(WIDE), len(WIDE), len(NEAR), len(WIDE), len(ALONG), len(ALONG), nx - 1, nx - 1):
+        for n in (len(NEAR), len(NEAR), len(WIDE), len(WIDE), len(NEAR), len(WIDE), len(ALONG), len(ALONG), nx - 1, nx - 1, nx):
             sems += [pltpu.SemaphoreType.DMA((n,)), pltpu.SemaphoreType.DMA((n,))]
         fine = (10, 2, 40, LANES)
         return pl.pallas_call(
@@ -719,7 +743,7 @@
                 v(2, *fine), v(3, 10, 32, LANES), v(3, 5, 24, LANES),
                 v(4, 21, 40, LANES), v(20, 40, LANES), v(12, 10, 40, LANES), v(2, 10, 40, LANES), v(2, 10, 40, LANES),
                 v(2, 10, 40, LANES), v(2, 10, 40, LANES), v(10, 40, LANES), v(10, 16, LANES), v(10, 32, LANES),
-                v(4, 48, LANES), v(48, LANES), v(16, 4, 48, LANES), v(16, 48, LANES), v(6, 10, 64, LANES),
+                v(3, 48, LANES), v(48, LANES), v(16, 3, 48, LANES), v(16, 48, LANES), v(6, 10, 64, LANES),
                 v(12, 8, 64, LANES), v(2, 8, 64, LANES), v(2, 8, 64, LANES), v(2, 10, 64, LANES), v(10, 40, LANES),
                 v(128, 2 * LANES),
                 pltpu.SemaphoreType.DMA((2,)), pltpu.SemaphoreType.DMA((2,)),

time: 80.7 us -> 52.5 us (0.65)
  Pallas kernels: 76.8 us -> 48.7 us
    pallas_call x1, Pallas kernels: 76.8 us -> 48.7 us  [local(): pl.pallas_call(functools.partial(kernel, nx, ny), out_shape=[jax.ShapeDty...]
where the time goes in v2:
time: 52.5 us; the launch traced here: 52.4 us
  Pallas kernels  48.7 us (93%)
  local copies, waits for them, and re-layouts  3.11 us (6%)
  between operations  0.65 us (1%)
    pallas_call x1, Pallas kernels, local(): pl.pallas_call(functools.partial(kernel, nx, ny), out_shape=[jax.ShapeDty...  48.7 us
    unnamed x6, local copies, waits for them, and re-layouts  3.11 us

profile of v2, /device:TPU:65, one launch (start us, length us, event | category | flops | bytes accessed | tf_op | source)
XLA Modules:
  0.0 52.4 jit_solution(6736150078515536083)
XLA Ops:
  0.6 0.0 copy-start
  0.6 0.9 %copy-done = f32[8,16,192]{2,1,0:T(8,128)S(1)} copy-done((f32[8,16,192]{2,1,0:T(8,128)S(1)}, f32[8,16,192]{2,1,0:T(8,128)}, u32[]{:S(2)}) %copy-start) | copy-done | bytes 98328
  1.5 0.0 copy-start.1
  1.5 0.9 %copy-done.1 = s32[8,16,192]{2,1,0:T(8,128)S(1)} copy-done((s32[8,16,192]{2,1,0:T(8,128)S(1)}, s32[8,16,192]{2,1,0:T(8,128)}, u32[]{:S(2)}) %copy-start.1) | copy-done | bytes 98328
  2.4 48.7 %shard_map.41 = (f32[8,16,192]{2,1,0:T(8,128)S(1)}, f32[8,16,192]{2,1,0:T(8,128)S(1)}) custom-call(f32[8,16,192]{2,1,0:T(8,128)S(1)} %copy-done, s32[8,16,192]{2,1,0:T(8,128)S(1)} %copy-done.1), custom_call_target="tpu_custom_call" | custom-call | tf_op jit(solution)/shard_map/pallas_call | solution.py:735
  51.1 0.7 %copy.6 = f32[8,16,192]{2,1,0:T(8,128)} copy(f32[8,16,192]{2,1,0:T(8,128)S(1)} %get-tuple-element.4) | data formatting | bytes 196608
  51.8 0.7 %copy.7 = f32[8,16,192]{2,1,0:T(8,128)} copy(f32[8,16,192]{2,1,0:T(8,128)S(1)} %get-tuple-element.5) | data formatting | bytes 196608
Async XLA Ops:
  0.6 0.9 %copy-start = (f32[8,16,192]{2,1,0:T(8,128)S(1)}, f32[8,16,192]{2,1,0:T(8,128)}, u32[]{:S(2)}) copy-start(f32[8,16,192]{2,1,0:T(8,128)} %rs_hbm.1) | copy-start | bytes 294916
  1.5 0.9 %copy-start.1 = (s32[8,16,192]{2,1,0:T(8,128)S(1)}, s32[8,16,192]{2,1,0:T(8,128)}, u32[]{:S(2)}) copy-start(s32[8,16,192]{2,1,0:T(8,128)} %ph_hbm.1) | copy-start | bytes 294916

commit v3 on v2

--- a/solution.py
+++ b/solution.py
@@ -42,12 +42,12 @@
 
 def kernel(
     nx, ny,
-    rs_hbm, ph_hbm, p_hbm, r_hbm,
-    rs_in, ph_in, out_p, out_r,
+    rs_hbm, ph_hbm, out_p, out_r,
+    rs_in, ph_in,
     ph, rs, wf, sf, df, rdf, pf, pb0, rf, tf, f1o,
     f1, b1, wm, sm, dm, rdm, pm, mb0, rm, em,
     lw, lb, gw, gb, ul, wl, sl, rdl, plow, e1, xo_s,
-    in_sem, out_sem,
+    in_sem,
     s_ph, r_ph, s_rs, r_rs, s_f1, r_f1, s_b1, r_b1, s_pb, r_pb, s_mb, r_mb,
     s_lw, r_lw, s_lb, r_lb, s_gw, r_gw, s_gb, r_gb, s_re, r_re,
 ):
@@ -116,8 +116,8 @@
 
     def fine_refs(arr, lead, pairs, rows):
         def refs(dx, dy):
-            x0, xn = span(dx, 3, 4, pairs)
-            y0, yn = span(dy, 8, 16, rows)
+            x0, xn = span(dx, 3, 4, 2 if dy else pairs)
+            y0, yn = span(dy, 8, 16, rows - 1 if dx else rows)
             pre = (slice(None),) * lead
             return (
                 arr.at[pre + (pl.ds(x0, xn), slice(None), pl.ds(y0, yn))],
@@ -126,10 +126,10 @@
 
         return refs
 
-    def mid_refs(arr, lead, own, size, far, rows):
+    def mid_refs(arr, lead, own, size, far, rows, far_corner):
         def refs(dx, dy):
-            x0, xn = span(dx, own, size, size if abs(dx) < 2 else far)
-            y0, yn = span(dy, 16, 8, rows)
+            x0, xn = span(dx, own, size, size if abs(dx) < 2 else far_corner[0] if dy else far)
+            y0, yn = span(dy, 16, 8, rows[0] if dx == 0 else rows[1] if abs(dx) < 2 else far_corner[1])
             pre = (slice(None),) * lead
             return (
                 arr.at[pre + (pl.ds(x0, xn), pl.ds(y0, yn))],
@@ -148,9 +148,9 @@
     ph_refs = fine_refs(ph, 1, 3, 5)
     rs_refs = fine_refs(rs, 1, 2, 4)
     pb_refs = fine_refs(pb0, 0, 3, 5)
-    f1_refs = mid_refs(f1, 1, 8, 4, (3, 2), (7, 6))
-    b1_refs = mid_refs(b1, 0, 8, 4, 2, 6)
-    mb_refs = mid_refs(mb0, 0, 4, 2, 2, 7)
+    f1_refs = mid_refs(f1, 1, 8, 4, (3, 2), ((7, 6), (6, 5)), (2, 2))
+    b1_refs = mid_refs(b1, 0, 8, 4, 2, (6, 5), (1, 1))
+    mb_refs = mid_refs(mb0, 0, 4, 2, 2, (7, 6), (1, 2))
     lw_refs = low_refs(lw, 1)
     lb_refs = low_refs(lb, 0)
     gy_steps = [(0, d) for d in ALONG]
@@ -335,10 +335,9 @@
         fy, fyn = f1o[1, i, 2:10, :], f1o[1, i, 3:11, :]
         fz = f1o[2, i, 2:10, :]
         fzn = jnp.where(h8, rot(fz, 63), rot(fz, 64))
-        f1[0, 8 + i, 16:24, :] = fx
-        f1[1, 8 + i, 16:24, :] = fy
-        f1[2, 8 + i, 16:24, :] = fz
-        f1[3, 8 + i, 16:24, :] = ((((fx + fxn) + fy) + fyn) + fz) + fzn
+        dg = ((((fx + fxn) + fy) + fyn) + fz) + fzn
+        for f, w in enumerate((fx, fy, fz)):
+            f1[f, 8 + i, 16:24, :] = jnp.where(lane_ok(8), w, rot(dg, 48 - 16 * f))
     send(NEAR, f1_refs, s_f1, r_f1)
 
     def zsum(v):
@@ -459,6 +458,8 @@
     def mid_weights(m0, m1, r0, n, top):
         odd, h1 = odd_mid(n, r0), h1_of(n)
         win, nxt = pl.ds(r0, n), pl.ds(r0 + 1, n)
+        q = lax.rem(iota(n, 1), 64)
+        q16, q32 = q < 16, q < 32
 
         def body(m, carry):
             valid = inside(n, 8 * b - 16 + r0, 8 * ny, pair_ok(2 * a - 4, m, 2 * nx))
@@ -469,7 +470,10 @@
             fz = [f1[2, e, win, :] for e in (e0, e1_)]
             zs = [jnp.where(h1, v, rot(v, 64)) for v in fz]
             zo = [jnp.where(h1, rot(v, 63), v) for v in fz]
-            dg = [f1[3, e, win, :] for e in (e0, e1_)]
+            dg = [
+                jnp.where(q16, rot(f1[0, e, win, :], 80), jnp.where(q32, rot(f1[1, e, win, :], 96), rot(f1[2, e, win, :], 112)))
+                for e in (e0, e1_)
+            ]
             for c in (0, 1):
                 def pick(v):
                     return jnp.where(odd, v[1 - c], v[c])
@@ -706,11 +710,7 @@
         out[...] = v.reshape(out.shape)
 
     join_from(pf, out_p)
-    put_p = pltpu.make_async_copy(out_p, p_hbm, out_sem.at[0])
-    put_p.start()
     join_from(rf, out_r)
-    put_r = pltpu.make_async_copy(out_r, r_hbm, out_sem.at[1])
-    put_r.start()
     for ok, cp in started:
         if ok is None:
             cp().wait_send()
@@ -718,8 +718,6 @@
             @pl.when(ok)
             def _():
                 cp().wait_send()
-    put_p.wait()
-    put_r.wait()
 
 
 def solution(mesh):
@@ -735,21 +733,21 @@
         return pl.pallas_call(
             functools.partial(kernel, nx, ny),
             out_shape=[jax.ShapeDtypeStruct(shape, F32)] * 2,
-            in_specs=[pl.BlockSpec(memory_space=pl.ANY)] * 2,
-            out_specs=[pl.BlockSpec(memory_space=pl.ANY)] * 2,
+            in_specs=[pl.BlockSpec(memory_space=pltpu.HBM)] * 2,
+            out_specs=[pl.BlockSpec(memory_space=pltpu.VMEM)] * 2,
             scratch_shapes=[
-                v(*shape), pltpu.VMEM(shape, jnp.int32), v(*shape), v(*shape),
+                v(*shape), pltpu.VMEM(shape, jnp.int32),
                 v(2, *fine), v(2, *fine), v(12, *fine), v(2, *fine), v(2, *fine), v(2, *fine), v(2, *fine), v(*fine),
                 v(2, *fine), v(3, 10, 32, LANES), v(3, 5, 24, LANES),
-                v(4, 21, 40, LANES), v(20, 40, LANES), v(12, 10, 40, LANES), v(2, 10, 40, LANES), v(2, 10, 40, LANES),
+                v(3, 21, 40, LANES), v(20, 40, LANES), v(12, 10, 40, LANES), v(2, 10, 40, LANES), v(2, 10, 40, LANES),
                 v(2, 10, 40, LANES), v(2, 10, 40, LANES), v(10, 40, LANES), v(10, 16, LANES), v(10, 32, LANES),
                 v(3, 48, LANES), v(48, LANES), v(16, 3, 48, LANES), v(16, 48, LANES), v(6, 10, 64, LANES),
                 v(12, 8, 64, LANES), v(2, 8, 64, LANES), v(2, 8, 64, LANES), v(2, 10, 64, LANES), v(10, 40, LANES),
                 v(128, 2 * LANES),
-                pltpu.SemaphoreType.DMA((2,)), pltpu.SemaphoreType.DMA((2,)),
+                pltpu.SemaphoreType.DMA((2,)),
             ] + sems,
             compiler_params=pltpu.CompilerParams(
-                collective_id=0, has_side_effects=True, vmem_limit_bytes=48 * 2**20
+                collective_id=0, has_side_effects=True, vmem_limit_bytes=63 * 2**20
             ),
         )(right_side, phase)
 

time: 52.5 us -> 46.6 us (0.89)
  Pallas kernels: 48.7 us -> 43.3 us
  local copies, waits for them, and re-layouts: 3.11 us -> 2.26 us
    pallas_call x1, Pallas kernels: 48.7 us -> 43.3 us  [local(): pl.pallas_call(functools.partial(kernel, nx, ny), out_shape=[jax.ShapeDty...]
    unnamed x6 -> x4, local copies, waits for them, and re-layouts: 3.11 us -> 2.26 us
where the time goes in v3:
time: 46.6 us; the launch traced here: 46.2 us
  Pallas kernels  43.3 us (93%)
  local copies, waits for them, and re-layouts  2.26 us (5%)
  between operations  0.65 us (1%)
    pallas_call x1, Pallas kernels, local(): pl.pallas_call(functools.partial(kernel, nx, ny), out_shape=[jax.ShapeDty...  43.3 us
    unnamed x4, local copies, waits for them, and re-layouts  2.26 us

profile of v3, /device:TPU:65, one launch (start us, length us, event | category | flops | bytes accessed | tf_op | source)
XLA Modules:
  0.0 46.2 jit_solution(3000487788796377878)
XLA Ops:
  0.6 43.3 %shard_map.41 = (f32[8,16,192]{2,1,0:T(8,128)}, f32[8,16,192]{2,1,0:T(8,128)}) custom-call(f32[8,16,192]{2,1,0:T(8,128)} %rs_hbm.1, s32[8,16,192]{2,1,0:T(8,128)} %ph_hbm.1), custom_call_target="tpu_custom_call" | custom-call | tf_op jit(solution)/shard_map/pallas_call | solution.py:733
  44.0 0.0 copy-start
  44.0 1.6 %copy.6 = f32[8,16,192]{2,1,0:T(8,128)} copy(f32[8,16,192]{2,1,0:T(8,128)} %get-tuple-element.4) | data formatting | bytes 196608
  45.6 0.0 copy-done
  45.6 0.7 %copy.7 = f32[8,16,192]{2,1,0:T(8,128)} copy(f32[8,16,192]{2,1,0:T(8,128)S(1)} %copy-done) | data formatting | bytes 196608
Async XLA Ops:
  44.0 1.6 %copy-start = (f32[8,16,192]{2,1,0:T(8,128)S(1)}, f32[8,16,192]{2,1,0:T(8,128)}, u32[]{:S(2)}) copy-start(f32[8,16,192]{2,1,0:T(8,128)} %get-tuple-element.5) | copy-start | bytes 294916

commit v4 on v3

--- a/solution.py
+++ b/solution.py
@@ -20,10 +20,15 @@
 W_DD = float(np.float32(2) * _D * _D / (_D + _D))
 
 REACH = 5
-NEAR = [(dx, dy) for dx in (-1, 0, 1) for dy in (-1, 0, 1) if (dx, dy) != (0, 0)]
+NEAR = [(-1, 0), (1, 0), (-1, -1), (1, -1), (-1, 1), (1, 1), (0, -1), (0, 1)]
 FAR = [(dx, dy) for dx in (-2, 2) for dy in (-1, 0, 1)]
 WIDE = NEAR + FAR
-ALONG = [d * s for d in range(1, REACH + 1) for s in (1, -1)]
+ALONG = [d * s for d in range(REACH, 0, -1) for s in (1, -1)]
+
+
+def ring_order(n):
+    side = 4
+    return sorted(range(1, n), key=lambda d: -(min(d % side, side - d % side) + min(d // side, side - d // side)))
 
 
 def rot(v, shift):
@@ -90,7 +95,7 @@
                 copy(src, dst, ssem, rsem, base + i, (a - dx, b - dy)).wait_recv()
 
     def ring_send(src, dst, ssem, rsem):
-        for d in range(1, nx):
+        for d in ring_order(nx):
             cp = functools.partial(copy, src, dst((4 - d) % nx), ssem, rsem, d - 1, (lax.rem(a + d, nx), b))
             cp().start()
             started.append((None, cp))
@@ -111,7 +116,7 @@
         copy(src, gw.at[i, :, pl.ds(24 - 24 * core, 20)], s_re, r_re, i, dev).wait_recv()
 
     def ring_arrive(src, dst, ssem, rsem):
-        for d in range(1, nx):
+        for d in ring_order(nx):
             copy(src, dst((4 - d) % nx), ssem, rsem, d - 1, (lax.rem(a + nx - d, nx), b)).wait_recv()
 
     def fine_refs(arr, lead, pairs, rows):
@@ -155,32 +160,24 @@
     lb_refs = low_refs(lb, 0)
     gy_steps = [(0, d) for d in ALONG]
 
+    bar = pltpu.get_barrier_semaphore()
+    count = jnp.int32(nx - 1)
+    for dx, dy in [(dx, dy) for dx, dy in WIDE if dy] + [(0, d) for d in ALONG if abs(d) > 1]:
+        ok = exists(dx, dy)
+
+        @pl.when(ok)
+        def _():
+            pl.semaphore_signal(bar, inc=1, device_id=(a + dx, b + dy), device_id_type=MESH)
+
+        count = count + ok.astype(jnp.int32)
+
+    for d in ring_order(nx):
+        pl.semaphore_signal(bar, inc=1, device_id=(lax.rem(a + d, nx), b), device_id_type=MESH)
     in_rs = pltpu.make_async_copy(rs_hbm, rs_in, in_sem.at[0])
     in_ph = pltpu.make_async_copy(ph_hbm, ph_in, in_sem.at[1])
     in_ph.start()
     in_rs.start()
 
-    bar = pltpu.get_barrier_semaphore()
-    greet = list(WIDE) + [(0, d) for d in ALONG if abs(d) > 1]
-    count = jnp.int32(0)
-    for dx, dy in greet:
-        ok = exists(dx, dy)
-
-        @pl.when(ok)
-        def _():
-            pl.semaphore_signal(bar, inc=1, device_id=(a + dx, b + dy), device_id_type=MESH)
-
-        count = count + ok.astype(jnp.int32)
-    for d in range(1, nx):
-        t = lax.rem(a + d, nx)
-        far = jnp.logical_or(t > a + 2, t < a - 2)
-
-        @pl.when(far)
-        def _():
-            pl.semaphore_signal(bar, inc=1, device_id=(t, b), device_id_type=MESH)
-
-        count = count + far.astype(jnp.int32)
-
     def iota(rows, dim):
         return lax.broadcasted_iota(jnp.int32, (rows, LANES), dim)
 
@@ -198,6 +195,11 @@
 
     def odd_low(rows, start):
         return lax.rem(iota(rows, 0) + start + iota(rows, 1), 2) == 1
+
+    def inverse(v):
+        r = pl.reciprocal(v, approx=True)
+        r = r * (2.0 - v * r)
+        return r * (2.0 - v * r)
 
     def zero(ref):
         ref[...] = jnp.zeros(ref.shape, F32)
@@ -240,6 +242,16 @@
     cc = lax.broadcasted_iota(jnp.int32, (nz, 2 * LANES), 1)
     q, hh, tt = lax.rem(cc, 64), lax.rem(lax.div(cc, 64), 2), lax.div(cc, 128)
     perm = jnp.where(jnp.logical_and(kk == 4 * q + 2 * hh + tt, q < 48), 1.0, 0.0).astype(F32)
+
+    def reorder(v, matrix):
+        m16 = matrix.astype(jnp.bfloat16)
+        total = None
+        for _ in range(3):
+            part = v.astype(jnp.bfloat16)
+            v = v - part.astype(F32)
+            dot = jnp.dot(part, m16, preferred_element_type=F32)
+            total = dot if total is None else total + dot
+        return total
 
     def split_into(values, dst):
         for t in (0, 1):
@@ -255,7 +267,7 @@
     split_into(jnp.dot(labels, perm, preferred_element_type=F32), ph)
     in_rs.wait()
     block = rs_in[...].reshape(128, nz)
-    split_into(jnp.dot(block, perm, precision=lax.Precision.HIGHEST, preferred_element_type=F32), rs)
+    split_into(reorder(block, perm), rs)
 
     pl.semaphore_wait(bar, count)
     send(NEAR, ph_refs, s_ph, r_ph)
@@ -290,35 +302,30 @@
 
     arrive(NEAR, ph_refs, s_ph, r_ph)
 
-    def fine_weights(m, carry):
-        valid = inside(RN, 16 * b - 8 + R0, 16 * ny, pair_ok(4 * a - 3, m, 4 * nx))
+    def levels(c, m, t):
+        dense = ph[c, m, t, pl.ds(R0, RN), :] > 0.5
+        return jnp.where(dense, W_DD, W_MX), jnp.where(dense, W_MX, W_LL)
+
+    def own_faces(m, carry):
         fx = fy = fz = None
         for t in (0, 1):
             both = []
             for c in (0, 1):
-                dense = ph[c, m, t, pl.ds(R0, RN), :] > 0.5
-                on = jnp.where(dense, W_DD, W_MX)
-                off = jnp.where(dense, W_MX, W_LL)
-                w = [jnp.where(s > 0.5, on, off) for s in fine_sides(ph, c, m, t, R0, RN, odd24[t], h24)]
-                dg = ((((w[0] + w[1]) + w[2]) + w[3]) + w[4]) + w[5]
-                rd = jnp.where(valid, 1.0 / dg, 0.0)
-                for f in range(6):
-                    wf[6 * c + f, m, t, pl.ds(R0, RN), :] = w[f] * rd
-                df[c, m, t, pl.ds(R0, RN), :] = dg
-                rdf[c, m, t, pl.ds(R0, RN), :] = rd
-                both.append(w)
-            x = jnp.where(odd24[t], both[1][1], both[0][1])
-            y = both[0][2] + both[1][2]
+                on, off = levels(c, m, t)
+                side = fine_sides(ph, c, m, t, R0, RN, odd24[t], h24)
+                both.append([jnp.where(side[f] > 0.5, on, off) for f in (1, 2, 5)])
+            x = jnp.where(odd24[t], both[1][0], both[0][0])
+            y = both[0][1] + both[1][1]
             fx = x if fx is None else fx + x
             fy = y if fy is None else fy + y
             if t == 0:
-                fz = both[0][5] + both[1][5]
+                fz = both[0][2] + both[1][2]
         tf[0, m, 0:RN, :] = fx
         tf[1, m, 0:RN, :] = fy
         tf[2, m, 0:RN, :] = fz
         return carry
 
-    lax.fori_loop(1, 9, fine_weights, 0)
+    lax.fori_loop(3, 8, own_faces, 0, unroll=True)
 
     even, oddr = pl.ds(0, 16, stride=2), pl.ds(1, 16, stride=2)
 
@@ -372,6 +379,24 @@
         v = jnp.where(lane_ok(8), jnp.where(h8, second, first), rot(inv, 48 - 16 * f))
         lw[f, 20:24, :] = v[0:4]
     send(gy_steps, lw_refs, s_lw, r_lw)
+
+    def fine_weights(m, carry):
+        valid = inside(RN, 16 * b - 8 + R0, 16 * ny, pair_ok(4 * a - 3, m, 4 * nx))
+        for t in (0, 1):
+            for c in (0, 1):
+                on, off = levels(c, m, t)
+                side = fine_sides(ph, c, m, t, R0, RN, odd24[t], h24)
+                many = ((((side[0] + side[1]) + side[2]) + side[3]) + side[4]) + side[5]
+                dg = 6.0 * off + many * (on - off)
+                rd = jnp.where(valid, inverse(dg), 0.0)
+                won, woff = on * rd, off * rd
+                for f in range(6):
+                    wf[6 * c + f, m, t, pl.ds(R0, RN), :] = jnp.where(side[f] > 0.5, won, woff)
+                df[c, m, t, pl.ds(R0, RN), :] = dg
+                rdf[c, m, t, pl.ds(R0, RN), :] = rd
+        return carry
+
+    lax.fori_loop(1, 9, fine_weights, 0, unroll=True)
 
     def fine_nb(c, m, t, r0, n, odd, h1):
         v = fine_sides(pf, c, m, t, r0, n, odd, h1)
@@ -651,8 +676,12 @@
             plow[c, s + 1, win, :] = total + wl[6 * c + 5, s, win, :] * rot(xs, 127)
             return carry
 
-        lax.fori_loop(0, 8, low_body, 0, unroll=True)
-        low_ghosts(c, r0, n)
+        side = (reach + 1) // 2
+        if side <= 3:
+            lax.fori_loop(4 - side, 5 + side, low_body, 0, unroll=True)
+        else:
+            lax.fori_loop(0, 8, low_body, 0, unroll=True)
+            low_ghosts(c, r0, n)
 
     arrive(WIDE, mb_refs, s_mb, r_mb)
     odd16, h16 = odd_low(16, 0), h1_of(16)
@@ -706,8 +735,7 @@
                 r, k = src[0, 3 + m, t, 8:24, :], src[1, 3 + m, t, 8:24, :]
                 xo_s[32 * m:32 * m + 16, t * LANES:(t + 1) * LANES] = jnp.where(odd, k, r)
                 xo_s[32 * m + 16:32 * m + 32, t * LANES:(t + 1) * LANES] = jnp.where(odd, r, k)
-        v = jnp.dot(xo_s[...], back, precision=lax.Precision.HIGHEST, preferred_element_type=F32)
-        out[...] = v.reshape(out.shape)
+        out[...] = reorder(xo_s[...], back).reshape(out.shape)
 
     join_from(pf, out_p)
     join_from(rf, out_r)
@@ -747,7 +775,7 @@
                 pltpu.SemaphoreType.DMA((2,)),
             ] + sems,
             compiler_params=pltpu.CompilerParams(
-                collective_id=0, has_side_effects=True, vmem_limit_bytes=63 * 2**20
+                collective_id=0, has_side_effects=True, vmem_limit_bytes=56262656
             ),
         )(right_side, phase)
 

time: 46.6 us -> 43.6 us (0.936)
  Pallas kernels: 43.3 us -> 41.4 us
  local copies, waits for them, and re-layouts: 2.26 us -> 1.31 us
    pallas_call x1, Pallas kernels: 43.3 us -> 41.4 us  [local(): pl.pallas_call(functools.partial(kernel, nx, ny), out_shape=[jax.ShapeDty...]
    unnamed x4 -> x2, local copies, waits for them, and re-layouts: 2.26 us -> 1.31 us
where the time goes in v4:
time: 43.6 us; the launch traced here: 43.3 us
  Pallas kernels  41.4 us (95%)
  local copies, waits for them, and re-layouts  1.31 us (3%)
  between operations  0.64 us (1%)
    pallas_call x1, Pallas kernels, local(): pl.pallas_call(functools.partial(kernel, nx, ny), out_shape=[jax.ShapeDty...  41.4 us
    unnamed x2, local copies, waits for them, and re-layouts  1.31 us

profile of v4, /device:TPU:65, one launch (start us, length us, event | category | flops | bytes accessed | tf_op | source)
XLA Modules:
  0.0 43.3 jit_solution(16911846978593098765)
XLA Ops:
  0.6 41.4 %shard_map.41 = (f32[8,16,192]{2,1,0:T(8,128)S(1)}, f32[8,16,192]{2,1,0:T(8,128)S(1)}) custom-call(f32[8,16,192]{2,1,0:T(8,128)} %rs_hbm.1, s32[8,16,192]{2,1,0:T(8,128)} %ph_hbm.1), custom_call_target="tpu_custom_call" | custom-call | tf_op jit(solution)/shard_map/pallas_call | solution.py:761
  42.0 0.7 %copy.6 = f32[8,16,192]{2,1,0:T(8,128)} copy(f32[8,16,192]{2,1,0:T(8,128)S(1)} %get-tuple-element.4) | data formatting | bytes 196608
  42.7 0.7 %copy.7 = f32[8,16,192]{2,1,0:T(8,128)} copy(f32[8,16,192]{2,1,0:T(8,128)S(1)} %get-tuple-element.5) | data formatting | bytes 196608

commit v5 on v4

--- a/solution.py
+++ b/solution.py
@@ -13,6 +13,7 @@
 MESH = pl.DeviceIdType.MESH
 LANES = 128
 BOTTOM = 8
+RING = 10
 
 _L, _D = np.float32(1.0), np.float32(0.1)
 W_LL = float(np.float32(2) * _L * _L / (_L + _L))
@@ -94,30 +95,51 @@
             def _():
                 copy(src, dst, ssem, rsem, base + i, (a - dx, b - dy)).wait_recv()
 
-    def ring_send(src, dst, ssem, rsem):
-        for d in ring_order(nx):
-            cp = functools.partial(copy, src, dst((4 - d) % nx), ssem, rsem, d - 1, (lax.rem(a + d, nx), b))
-            cp().start()
-            started.append((None, cp))
-
-    def relay_refs(i):
-        core = lax.rem(b, 2)
-        return gw.at[i, :, pl.ds(4 + 16 * core, 20)], gw.at[i, :, pl.ds(24 * core, 20)], (a, b + 1 - 2 * core)
-
-    def relay(i):
-        src, dst, dev = relay_refs(i)
-        cp = functools.partial(copy, src, dst, s_re, r_re, i, dev)
-        cp().start()
-        started.append((None, cp))
-
-    def relay_arrive(i):
-        src, dst, dev = relay_refs(i)
-        core = lax.rem(b, 2)
-        copy(src, gw.at[i, :, pl.ds(24 - 24 * core, 20)], s_re, r_re, i, dev).wait_recv()
-
-    def ring_arrive(src, dst, ssem, rsem):
-        for d in ring_order(nx):
-            copy(src, dst((4 - d) % nx), ssem, rsem, d - 1, (lax.rem(a + nx - d, nx), b)).wait_recv()
+    ring = [dx for d in ring_order(nx) for dx in (d, d - nx) if abs(dx) <= RING]
+    core = lax.rem(b, 2)
+
+    def slot(dx):
+        return (4 - dx) % nx
+
+    def whole_rows(dx):
+        return pl.ds(2 * abs(dx), 44 - 4 * abs(dx))
+
+    def half_rows(dx):
+        return pl.ds(2 * abs(dx) + core * (20 - 2 * abs(dx)), 24 - 2 * abs(dx))
+
+    def send_w(dx):
+        return copy(lw.at[:, half_rows(dx)], gw.at[slot(dx), :, half_rows(dx)], s_gw, r_gw, dx % nx - 1, (a + dx, b))
+
+    def send_b(dx):
+        return copy(lb.at[whole_rows(dx)], gb.at[slot(dx), whole_rows(dx)], s_gb, r_gb, dx % nx - 1, (a + dx, b))
+
+    def relay(dx):
+        d, n = 2 * abs(dx), 20 - 2 * abs(dx)
+        src, dst = d + 4 + core * (16 - d), d + core * (24 - d)
+        return copy(
+            gw.at[slot(dx), :, pl.ds(src, n)], gw.at[slot(dx), :, pl.ds(dst, n)], s_re, r_re, dx % nx, (a, b + 1 - 2 * core)
+        )
+
+    def relay_comes(dx):
+        d, n = 2 * abs(dx), 20 - 2 * abs(dx)
+        dst = pl.ds(24 + core * (d - 24), n)
+        return copy(
+            gw.at[slot(dx), :, dst], gw.at[slot(dx), :, dst], s_re, r_re, dx % nx, (a, b + 1 - 2 * core)
+        )
+
+    def ring_send(made):
+        for dx in ring:
+            @pl.when(exists(dx, 0))
+            def _():
+                made(dx).start()
+
+            started.append((exists(dx, 0), functools.partial(made, dx)))
+
+    def ring_arrive(made):
+        for dx in ring:
+            @pl.when(exists(-dx, 0))
+            def _():
+                made(dx).wait_recv()
 
     def fine_refs(arr, lead, pairs, rows):
         def refs(dx, dy):
@@ -236,6 +258,17 @@
         def _():
             zero(lw.at[:, pl.ds(20 + 4 * d, 4)])
             zero(lb.at[pl.ds(20 + 4 * d, 4)])
+
+    for dx in list(range(1, nx)) + list(range(-1, -nx, -1)):
+        @pl.when(exists(-dx, 0))
+        def _():
+            if abs(dx) > RING:
+                zero(gw.at[slot(dx)])
+                zero(gb.at[slot(dx)])
+            else:
+                for rows in (slice(0, 2 * abs(dx)), slice(44 - 2 * abs(dx), 48)):
+                    zero(gw.at[slot(dx), :, rows])
+                    zero(gb.at[slot(dx), rows])
 
     nz = rs_in.shape[2]
     kk = lax.broadcasted_iota(jnp.int32, (nz, 2 * LANES), 0)
@@ -555,8 +588,7 @@
     arrive(NEAR, f1_refs, s_f1, r_f1)
     mid_weights(2, 8, 12, 16, 15)
     arrive(gy_steps, lw_refs, s_lw, r_lw)
-    half_rows = pl.ds(20 * lax.rem(b, 2), 24)
-    ring_send(lw.at[:, half_rows], lambda i: gw.at[i, :, half_rows], s_gw, r_gw)
+    ring_send(send_w)
     arrive(NEAR, b1_refs, s_b1, r_b1)
     mid_source(2, 8, 12, 16, True)
     mid_half(1, 2, 8, 13, 16)
@@ -589,7 +621,7 @@
     mid_source(1, 9, 8, 24, False)
 
     arrive(gy_steps, lb_refs, s_lb, r_lb)
-    ring_send(lb.at[0:44], lambda i: gb.at[i, 0:44], s_gb, r_gb)
+    ring_send(send_b)
     gw[4, :, 0:44] = lw[:, 0:44]
     gb[4, 0:44] = lb[0:44]
 
@@ -604,13 +636,18 @@
             return jnp.where(h48, rot(hi, 64), lo)
         return jnp.where(h48, hi, rot(lo, 64))
 
-    ring_arrive(lw.at[:, half_rows], lambda i: gw.at[i, :, half_rows], s_gw, r_gw)
-    for i in range(nx):
-        if i != 4:
-            relay(i)
-    for i in range(nx):
-        if i != 4:
-            relay_arrive(i)
+    ring_arrive(send_w)
+    passed = [dx for dx in ring if abs(dx) < RING]
+    for dx in passed:
+        @pl.when(exists(-dx, 0))
+        def _():
+            relay(dx).start()
+
+        started.append((exists(-dx, 0), functools.partial(relay, dx)))
+    for dx in passed:
+        @pl.when(exists(-dx, 0))
+        def _():
+            relay_comes(dx).wait_recv()
 
     def low_weights(s, carry):
         u = [fold(gw[s, f // 2], gw[s + 8, f // 2], f % 2) for f in range(6)]
@@ -639,7 +676,7 @@
 
     lax.fori_loop(0, 8, low_black, 0, unroll=True)
 
-    ring_arrive(lb.at[0:44], lambda i: gb.at[i, 0:44], s_gb, r_gb)
+    ring_arrive(send_b)
 
     def low_source(s, carry):
         lo, hi = gb[s], gb[s + 8]

time: 43.6 us -> 39.3 us (0.901)
  the two profiles are of different devices: /device:TPU:65 before, /device:TPU:68 now
where the time goes in v5:
time: 39.3 us; the launch traced here: 39.2 us
  Pallas kernels  37.2 us (95%)
  local copies, waits for them, and re-layouts  1.31 us (3%)
  between operations  0.64 us (2%)
    pallas_call x1, Pallas kernels, local(): pl.pallas_call(functools.partial(kernel, nx, ny), out_shape=[jax.ShapeDty...  37.2 us
    unnamed x2, local copies, waits for them, and re-layouts  1.31 us

profile of v5, /device:TPU:68, one launch (start us, length us, event | category | flops | bytes accessed | tf_op | source)
XLA Modules:
  0.0 39.2 jit_solution(10064970343607260069)
XLA Ops:
  0.6 37.2 %shard_map.41 = (f32[8,16,192]{2,1,0:T(8,128)S(1)}, f32[8,16,192]{2,1,0:T(8,128)S(1)}) custom-call(f32[8,16,192]{2,1,0:T(8,128)} %rs_hbm.1, s32[8,16,192]{2,1,0:T(8,128)} %ph_hbm.1), custom_call_target="tpu_custom_call" | custom-call | tf_op jit(solution)/shard_map/pallas_call | solution.py:798
  37.9 0.7 %copy.6 = f32[8,16,192]{2,1,0:T(8,128)} copy(f32[8,16,192]{2,1,0:T(8,128)S(1)} %get-tuple-element.4) | data formatting | bytes 196608
  38.5 0.7 %copy.7 = f32[8,16,192]{2,1,0:T(8,128)} copy(f32[8,16,192]{2,1,0:T(8,128)S(1)} %get-tuple-element.5) | data formatting | bytes 196608

commit v6 on v5

--- a/solution.py
+++ b/solution.py
@@ -694,13 +694,12 @@
         plow[c, 9, win, :] = rot(plow[c, 1, win, :], 64)
 
     low_ghosts(0, 8, LR)
-    for half in range(2, 2 * BOTTOM + 1):
-        c = (half - 1) % 2
-        reach = 4 + 2 * BOTTOM - half
+    def low_half(c, first, step, times, reach):
         r0, n = 8 + 20 - reach, 8 * ((4 + 2 * reach + 7) // 8)
         odd = odd_low(n, r0)
 
-        def low_body(s, carry, c=c, r0=r0, n=n, odd=odd):
+        def low_body(i, carry):
+            s = first + step * i
             o = 1 - c
             win = pl.ds(r0, n)
             xs, lo, hi = plow[o, s + 1, win, :], plow[o, s, win, :], plow[o, s + 2, win, :]
@@ -713,12 +712,19 @@
             plow[c, s + 1, win, :] = total + wl[6 * c + 5, s, win, :] * rot(xs, 127)
             return carry
 
-        side = (reach + 1) // 2
-        if side <= 3:
-            lax.fori_loop(4 - side, 5 + side, low_body, 0, unroll=True)
-        else:
-            lax.fori_loop(0, 8, low_body, 0, unroll=True)
-            low_ghosts(c, r0, n)
+        lax.fori_loop(0, times, low_body, 0, unroll=True)
+        return r0, n
+
+    for half in range(2, 2 * BOTTOM + 1):
+        c = (half - 1) % 2
+        reach = 4 + 2 * BOTTOM - half
+        low_half(c, 4, 1, 1, reach)
+        for far in (1, 2, 3):
+            if reach >= 2 * far - 1:
+                win = low_half(c, 4 - far, 2 * far, 2, reach - 2 * far + 1)
+        if reach >= 7:
+            low_half(c, 0, 1, 1, reach - 7)
+            low_ghosts(c, *win)
 
     arrive(WIDE, mb_refs, s_mb, r_mb)
     odd16, h16 = odd_low(16, 0), h1_of(16)

time: 39.3 us -> 39.1 us (level)
  no operation moved by 1% of the time
where the time goes in v6:
time: 39.1 us; the launch traced here: 39 us
  Pallas kernels  37 us (95%)
  local copies, waits for them, and re-layouts  1.31 us (3%)
  between operations  0.64 us (2%)
    pallas_call x1, Pallas kernels, local(): pl.pallas_call(functools.partial(kernel, nx, ny), out_shape=[jax.ShapeDty...  37 us
    unnamed x2, local copies, waits for them, and re-layouts  1.31 us

profile of v6, /device:TPU:68, one launch (start us, length us, event | category | flops | bytes accessed | tf_op | source)
XLA Modules:
  0.0 39.0 jit_solution(15492689825097198532)
XLA Ops:
  0.6 37.0 %shard_map.41 = (f32[8,16,192]{2,1,0:T(8,128)S(1)}, f32[8,16,192]{2,1,0:T(8,128)S(1)}) custom-call(f32[8,16,192]{2,1,0:T(8,128)} %rs_hbm.1, s32[8,16,192]{2,1,0:T(8,128)} %ph_hbm.1), custom_call_target="tpu_custom_call" | custom-call | tf_op jit(solution)/shard_map/pallas_call | solution.py:804
  37.6 0.7 %copy.6 = f32[8,16,192]{2,1,0:T(8,128)} copy(f32[8,16,192]{2,1,0:T(8,128)S(1)} %get-tuple-element.4) | data formatting | bytes 196608
  38.3 0.7 %copy.7 = f32[8,16,192]{2,1,0:T(8,128)} copy(f32[8,16,192]{2,1,0:T(8,128)S(1)} %get-tuple-element.5) | data formatting | bytes 196608

commit v7 on v6

--- a/solution.py
+++ b/solution.py
@@ -585,10 +585,10 @@
 
         lax.fori_loop(m0, m1, body, 0, unroll=True)
 
+    arrive(gy_steps, lw_refs, s_lw, r_lw)
+    ring_send(send_w)
     arrive(NEAR, f1_refs, s_f1, r_f1)
     mid_weights(2, 8, 12, 16, 15)
-    arrive(gy_steps, lw_refs, s_lw, r_lw)
-    ring_send(send_w)
     arrive(NEAR, b1_refs, s_b1, r_b1)
     mid_source(2, 8, 12, 16, True)
     mid_half(1, 2, 8, 13, 16)

time: 39.1 us -> 39.1 us (level)
  no operation moved by 1% of the time
where the time goes in v7:
time: 39.1 us; the launch traced here: 39 us
  Pallas kernels  37 us (95%)
  local copies, waits for them, and re-layouts  1.31 us (3%)
  between operations  0.64 us (2%)
    pallas_call x1, Pallas kernels, local(): pl.pallas_call(functools.partial(kernel, nx, ny), out_shape=[jax.ShapeDty...  37 us
    unnamed x2, local copies, waits for them, and re-layouts  1.31 us

profile of v7, /device:TPU:68, one launch (start us, length us, event | category | flops | bytes accessed | tf_op | source)
XLA Modules:
  0.0 39.0 jit_solution(10459073226382182360)
XLA Ops:
  0.6 37.0 %shard_map.41 = (f32[8,16,192]{2,1,0:T(8,128)S(1)}, f32[8,16,192]{2,1,0:T(8,128)S(1)}) custom-call(f32[8,16,192]{2,1,0:T(8,128)} %rs_hbm.1, s32[8,16,192]{2,1,0:T(8,128)} %ph_hbm.1), custom_call_target="tpu_custom_call" | custom-call | tf_op jit(solution)/shard_map/pallas_call | solution.py:804
  37.6 0.7 %copy.6 = f32[8,16,192]{2,1,0:T(8,128)} copy(f32[8,16,192]{2,1,0:T(8,128)S(1)} %get-tuple-element.4) | data formatting | bytes 196608
  38.3 0.7 %copy.7 = f32[8,16,192]{2,1,0:T(8,128)} copy(f32[8,16,192]{2,1,0:T(8,128)S(1)} %get-tuple-element.5) | data formatting | bytes 196608
